TPU v7x, 512 devices: a whole 4x8x8 slice. The times are simulated.
512 devices in a mesh: bfly: 32 (over y, x), sec: 2 (over core), probe: 8 (over z).
Axes of the slice: x: 4, y: 8, z: 8, core: 2. Of those that a mesh axis runs over, the one named last changes fastest.
Arguments:
- probes: bfloat16 [512, 1024, 256], P('bfly', 'probe'), may hold values from -6 to 6
- mixers: bfloat16 [9, 2, 256, 256], replicated, may hold values from -0.25 to 0.25
- box_gains: float32 [4, 512, 256], P(None, 'bfly'), may hold values from 0.1 to 1.9
- box_orders: int32 [4, 512], P(None, 'bfly'), may hold values from 0 to 15, as said below
- near_count: int32 [512], P('bfly'), may hold values from 1 to 6, as said below
- near_cols: int32 [512, 6], P('bfly'), may hold values from 0 to 511, as said below
- near_scale: float32 [512, 6, 256], P('bfly'), may hold values from 0.1 to 1.9
- near_table: bfloat16 [6, 256, 256], P(None, 'probe'), may hold values from -0.1875 to 0.1875
Outputs:
- response: float32 [512, 1024, 256], P('bfly', 'probe')
Inputs may be any that keep to these rules, and one draw needn't show every extreme that they name: `box_orders`: each aligned block of 16 entries of a row is a permutation of 0 to 15. `near_count`: some box row has 6 blocks. `near_cols`: each block's box lies within 8 boxes of its row's box.
All inputs are finite; a program needn't handle non-finite values.
Results may differ from a plain program's by a relative error of at most 0.02.
Values may be sent and summed in bfloat16 or wider, within the bound.
No kernel may reach another device: no remote copies, remote signals or barrier semaphores. Data moves between devices by JAX's collectives and lax.ppermute only.
A program may use at most 64 MiB of HBM per device.

v0:
```python
import jax
import jax.numpy as jnp
from jax import lax
from jax.sharding import PartitionSpec as P

LOCAL = 4
MAXB = 6
RIM = 8


def from_partner(block, axis, stride):
    count = lax.axis_size(axis)
    route = []
    for low in range(count):
        high = low | 1 << stride
        if high != low and high < count:
            route += [(low, high), (high, low)]
    return lax.ppermute(block, axis, route)


def extended_2(block, sides, width):
    for axis, dim in sides:
        count = lax.axis_size(axis)
        forward = [(i, i + 1) for i in range(count - 1)]
        backward = [(target, source) for source, target in forward]
        low = lax.ppermute(
            lax.slice_in_dim(block, block.shape[dim] - width, None, axis=dim), axis, forward
        )
        high = lax.ppermute(lax.slice_in_dim(block, 0, width, axis=dim), axis, backward)
        block = jnp.concatenate([low, block, high], axis=dim)
    return block


def pair_level(current, stride, weights):
    full_shape = current.shape
    grouped = current.reshape(
        full_shape[0] // (2 * stride), 2, stride, full_shape[1], full_shape[2]
    )
    partner = grouped[:, ::-1].reshape(full_shape)
    own_rows = current.reshape(-1, full_shape[2])
    other_rows = partner.reshape(-1, full_shape[2])
    product = jnp.dot(own_rows, weights[0], preferred_element_type=jnp.float32)
    product = product + jnp.dot(other_rows, weights[1], preferred_element_type=jnp.float32)
    return product.reshape(full_shape)


def gated(flag, active_fn, resting_fn, operand_value):
    return lax.cond(flag, active_fn, resting_fn, operand_value)


def keep_same(values):
    return values


def shards(probes, mixers, box_gains, box_orders, near_count, near_cols, near_scale, near_table):
    box_count, probe_count, feature_count = probes.shape
    peer_count = lax.axis_size("bfly")
    cross_count = peer_count.bit_length() - 1
    is_far = lax.axis_index("sec") == 0

    def local_levels(values):
        for level_index in range(LOCAL):
            values = jnp.take(values, box_orders[level_index], axis=0)
            mixed = pair_level(values, 2**level_index, mixers[level_index])
            values = (mixed * box_gains[level_index][:, None, :]).astype(jnp.bfloat16)
        return values

    current = gated(is_far, local_levels, keep_same, probes)
    column_count = current.shape[1]
    for bit_index in range(cross_count):
        weights = mixers[LOCAL + bit_index]
        partner = from_partner(current, "bfly", bit_index)

        def combine_pair(both, weights=weights):
            own_part = jnp.dot(
                both[0].reshape(-1, feature_count), weights[0], preferred_element_type=jnp.float32
            )
            summed = own_part + jnp.dot(
                both[1].reshape(-1, feature_count), weights[1], preferred_element_type=jnp.float32
            )
            return summed.reshape(both[0].shape).astype(jnp.bfloat16)

        def first_only(both):
            return both[0]

        current = gated(is_far, combine_pair, first_only, (current, partner))
    far_value = current.astype(jnp.float32)
    flag = jnp.logical_not(is_far)
    device_index = lax.axis_index("bfly")
    column_count = probes.shape[1]
    extended = extended_2(probes, (("bfly", 0),), RIM)

    def build_operand(extended_rows):
        local_cols = near_cols - (device_index * box_count - RIM)
        gathered = jnp.take(extended_rows, local_cols.reshape(-1), axis=0).reshape(
            box_count, MAXB, column_count, feature_count
        )
        active = jnp.arange(MAXB, dtype=jnp.int32)[None, :] < near_count[:, None]
        scaling = near_scale * active[:, :, None].astype(jnp.float32)
        return (gathered.astype(jnp.float32) * scaling[:, :, None, :]).astype(jnp.bfloat16)

    def empty_operand(extended_rows):
        return jnp.zeros((box_count, MAXB, column_count, feature_count), jnp.bfloat16)

    operand = gated(flag, build_operand, empty_operand, extended)
    initial = jnp.zeros((box_count, column_count, feature_count), jnp.float32)
    table_piece = lax.all_gather(near_table, "probe", axis=1, tiled=True)

    def add_product(running):
        return jnp.einsum("bkpw,kwv->bpv", operand, table_piece, preferred_element_type=jnp.float32)

    near_value = gated(flag, add_product, keep_same, initial)
    section_term = jnp.where(is_far, far_value, near_value)
    return lax.psum(section_term.astype(jnp.bfloat16), "sec").astype(jnp.float32)


def solution(mesh):
    return jax.shard_map(
        shards,
        mesh=mesh,
        in_specs=(
            P("bfly", "probe", None),
            P(),
            P(None, "bfly", None),
            P(None, "bfly"),
            P("bfly"),
            P("bfly", None),
            P("bfly", None, None),
            P(None, "probe", None),
        ),
        out_specs=P("bfly", "probe", None),
        check_vma=False,
    )
```

profile of v0, /device:TPU:1, one launch (start us, length us, event | category | flops | bytes accessed | tf_op | source)
XLA Modules:
  0.0 255.7 jit_solution(360368745469500119)
XLA Ops:
  6.5 0.0 all-reduce.2.cloned.1.call-start
  6.5 1.2 conditional.8
  6.5 1.2 copy.24
  7.8 3.9 %collective-permute-start = (bf16[16,128,256]{2,1,0:T(8,128)(2,1)S(1)}, bf16[16,128,256]{2,1,0:T(8,128)(2,1)S(1)}, u32[]{:S(2)}, u32[]{:S(2)}) collective-permute-start(bf16[16,128,256]{2,1,0:T(8,128)(2,1)S(1)} %get-tuple-element.176), channel_id=1, source_target_pairs={{0,16},{16,0},{32,48},{48,32},{64,80},{80,64},{96,112},{112,96},{1... | collective-permute-start | bytes 3145736 | tf_op jit(solution)/shard_map/ppermute | solution.py:18
  11.7 12.2 %collective-permute-done = bf16[16,128,256]{2,1,0:T(8,128)(2,1)S(1)} collective-permute-done((bf16[16,128,256]{2,1,0:T(8,128)(2,1)S(1)}, bf16[16,128,256]{2,1,0:T(8,128)(2,1)S(1)}, u32[]{:S(2)}, u32[]{:S(2)}) %collective-permute-start) | collective-permute-done | bytes 1048608 | tf_op jit(solution)/shard_map/ppermute | solution.py:18
  23.9 4.9 %collective-permute-start.1 = (bf16[16,128,256]{2,1,0:T(8,128)(2,1)S(1)}, bf16[16,128,256]{2,1,0:T(8,128)(2,1)S(1)}, u32[]{:S(2)}, u32[]{:S(2)}) collective-permute-start(bf16[16,128,256]{2,1,0:T(8,128)(2,1)S(1)} %get-tuple-element.177), channel_id=1, source_target_pairs={{0,32},{32,0},{16,48},{48,16},{64,96},{96,64},{80,112},{112,80},{1... | collective-permute-start | bytes 3145736 | tf_op jit(solution)/shard_map/ppermute | solution.py:18
  28.8 15.5 %collective-permute-done.1 = bf16[16,128,256]{2,1,0:T(8,128)(2,1)S(1)} collective-permute-done((bf16[16,128,256]{2,1,0:T(8,128)(2,1)S(1)}, bf16[16,128,256]{2,1,0:T(8,128)(2,1)S(1)}, u32[]{:S(2)}, u32[]{:S(2)}) %collective-permute-start.1) | collective-permute-done | bytes 1048608 | tf_op jit(solution)/shard_map/ppermute | solution.py:18
  44.3 5.2 %collective-permute-start.2 = (bf16[16,128,256]{2,1,0:T(8,128)(2,1)S(1)}, bf16[16,128,256]{2,1,0:T(8,128)(2,1)S(1)}, u32[]{:S(2)}, u32[]{:S(2)}) collective-permute-start(bf16[16,128,256]{2,1,0:T(8,128)(2,1)S(1)} %get-tuple-element.178), channel_id=1, source_target_pairs={{0,64},{64,0},{16,80},{80,16},{32,96},{96,32},{48,112},{112,48},{1... | collective-permute-start | bytes 3145736 | tf_op jit(solution)/shard_map/ppermute | solution.py:18
  49.5 12.2 %collective-permute-done.2 = bf16[16,128,256]{2,1,0:T(8,128)(2,1)S(1)} collective-permute-done((bf16[16,128,256]{2,1,0:T(8,128)(2,1)S(1)}, bf16[16,128,256]{2,1,0:T(8,128)(2,1)S(1)}, u32[]{:S(2)}, u32[]{:S(2)}) %collective-permute-start.2) | collective-permute-done | bytes 1048608 | tf_op jit(solution)/shard_map/ppermute | solution.py:18
  61.6 4.4 %collective-permute-start.3 = (bf16[16,128,256]{2,1,0:T(8,128)(2,1)S(1)}, bf16[16,128,256]{2,1,0:T(8,128)(2,1)S(1)}, u32[]{:S(2)}, u32[]{:S(2)}) collective-permute-start(bf16[16,128,256]{2,1,0:T(8,128)(2,1)S(1)} %get-tuple-element.179), channel_id=1, source_target_pairs={{0,128},{128,0},{16,144},{144,16},{32,160},{160,32},{48,176},{176,... | collective-permute-start | bytes 3145736 | tf_op jit(solution)/shard_map/ppermute | solution.py:18
  66.0 23.5 %collective-permute-done.3 = bf16[16,128,256]{2,1,0:T(8,128)(2,1)S(1)} collective-permute-done((bf16[16,128,256]{2,1,0:T(8,128)(2,1)S(1)}, bf16[16,128,256]{2,1,0:T(8,128)(2,1)S(1)}, u32[]{:S(2)}, u32[]{:S(2)}) %collective-permute-start.3) | collective-permute-done | bytes 1048608 | tf_op jit(solution)/shard_map/ppermute | solution.py:18
  89.5 0.0 copy-start
  89.5 0.0 copy-start.2
  89.5 7.6 %collective-permute-start.4 = (bf16[16,128,256]{2,1,0:T(8,128)(2,1)S(1)}, bf16[16,128,256]{2,1,0:T(8,128)(2,1)}, u32[]{:S(2)}, u32[]{:S(2)}) collective-permute-start(bf16[16,128,256]{2,1,0:T(8,128)(2,1)S(1)} %get-tuple-element.180), channel_id=1, source_target_pairs={{0,256},{256,0},{16,272},{272,16},{32,288},{288,32},{48,304},{304,... | collective-permute-start | bytes 3145736 | tf_op jit(solution)/shard_map/ppermute | solution.py:18
  97.1 0.0 copy-done
  97.1 0.1 fusion.53
  97.2 1.3 collective-permute-start.6
  98.5 4.8 %collective-permute-start.5 = (bf16[8,128,256]{2,1,0:T(8,128)(2,1)S(1)}, bf16[8,128,256]{2,1,0:T(8,128)(2,1)}, u32[]{:S(2)}, u32[]{:S(2)}) collective-permute-start(bf16[8,128,256]{2,1,0:T(8,128)(2,1)S(1)} %get-tuple-element.174), channel_id=1, source_target_pairs={{0,16},{16,32},{32,48},{48,64},{64,80},{80,96},{96,112},{112,128},... | collective-permute-start | bytes 1572872 | tf_op jit(solution)/shard_map/ppermute | solution.py:26
  103.3 0.0 copy-done.2
  103.3 27.7 %all_gather.3 = bf16[6,256,256]{2,1,0:T(8,128)(2,1)} all-gather(bf16[6,32,256]{2,1,0:T(8,128)(2,1)S(1)} %copy-done.2), channel_id=1, replica_groups=mesh['bfly'=32,'sec'=2,'probe'=8] {'probe'}, dimensions={1}, use_global_device_ids=true | all-gather | bytes 884736 | tf_op jit(solution)/shard_map/all_gather | solution.py:107
  131.0 0.0 copy-start.3
  131.0 0.0 copy-start.5
  131.0 0.0 copy-start.6
  131.0 0.0 collective-permute-done.6
  131.0 0.0 copy-start.1
  131.0 0.8 copy-done.1
  131.8 0.0 collective-permute-done.5
  131.8 1.8 pad_maximum_fusion
  133.6 0.0 copy-done.3
  133.6 0.0 copy-done.5
  133.6 0.0 copy-done.6
  133.6 15.4 %conditional.14 = (bf16[16,6,128,256]{3,2,1,0:T(8,128)(2,1)}) conditional(s32[]{:T(128)} %convert_element_type.85, () %tuple.71, (s32[]{:T(128)}, s32[16,6]{0,1:T(8,128)S(1)}, bf16[32,128,256]{2,1,0:T(8,128)(2,1)S(1)}, s32[16]{0:T(128)S(1)}, f32[16,6,256]{2,0,1:T(8,128)S(1)}) %tuple.113), branch_computations={%region_12.14_spmd, %region_13.15_spmd} | conditional | flops 12609666 | bytes 25469732 | solution.py:48
  133.8 0.1 fusion.31
  133.9 0.1 copy_multiply_fusion
  134.0 0.1 copy.16
  134.1 0.1 reshape.180
  134.2 6.0 %gather_fusion = bf16[96,128,256]{2,1,0:T(8,128)(2,1)} fusion(bf16[32,128,256]{2,1,0:T(8,128)(2,1)S(1)} %get-tuple-element.117, s32[1024]{0:T(1024)S(1)} %pad_clamp_fusion), kind=kCustom, calls=%fused_computation.1 | custom fusion | bytes 12583296 | tf_op jit(solution)/shard_map/cond/branch_1_fun/jit(_take)/gather | solution.py:95
  140.2 8.9 %multiply_convert_fusion = bf16[16,6,128,256]{3,2,1,0:T(8,128)(2,1)} fusion(f32[16,6,256]{2,1,0:T(8,128)S(1)} %copy_multiply_fusion, bf16[16,6,128,256]{3,2,1,0:T(8,128)(2,1)} %bitcast.143, pred[16,6]{1,0:T(8,128)(4,1)S(1)} %get-tuple-element.150), kind=kLoop, calls=%fused_computation.42 | loop fusion | flops 12582912 | bytes 12681312 | tf_op jit(solution)/shard_map/cond/branch_1_fun/convert_element_type | solution.py:100
  149.1 4.7 %conditional.15 = (bf16[16,128,256]{2,1,0:T(8,128)(2,1)S(1)}) conditional(s32[]{:T(128)} %convert_element_type.85, () %tuple.70, (bf16[16,6,128,256]{3,2,1,0:T(8,128)(2,1)}, bf16[6,256,256]{2,1,0:T(8,128)(2,1)}) %tuple.73), branch_computations={%region_14.16_spmd, %region_15.17_spmd} | conditional | flops 1610612736 | bytes 8126472 | solution.py:48
  149.1 4.7 %convolution_bitcast_fusion = bf16[16,128,256]{2,1,0:T(8,128)(2,1)S(1)} fusion(bf16[16,6,128,256]{3,2,1,0:T(8,128)(2,1)} %get-tuple-element.120, bf16[6,256,256]{2,1,0:T(8,128)(2,1)} %get-tuple-element.121), kind=kOutput, calls=%fused_computation.40 | convolution fusion | flops 1610612736 | bytes 8126464 | tf_op jit(solution)/shard_map/cond/branch_1_fun/bkpw,kwv->bpv/dot_general | solution.py:110
  153.8 0.0 collective-permute-done.4
  153.8 1.3 select_convert_fusion
  155.1 0.0 all-reduce.2.cloned.1.call-update
  155.1 90.9 %all-reduce.2.cloned.1.call-done = bf16[16,128,256]{2,1,0:T(8,128)(2,1)} async-done(((bf16[16,128,256]{2,1,0:T(8,128)(2,1)}), bf16[16,128,256]{2,1,0:T(8,128)(2,1)}) %all-reduce.2.cloned.1.call-update) | async-done | bytes 1048592 | tf_op jit(solution)/shard_map/psum | solution.py:114
  246.1 2.8 %convert_element_type.87 = f32[16,128,256]{2,1,0:T(8,128)} convert(bf16[16,128,256]{2,1,0:T(8,128)(2,1)} %all-reduce.2.cloned.1.call-done) | non-fusion elementwise | flops 524288 | bytes 3145728 | tf_op jit(solution)/shard_map/convert_element_type | solution.py:114
  (8 shorter events, 0.0 us)
Async XLA Ops:
  6.5 239.5 %all-reduce.2.cloned.1.call-start = ((), (), s32[]{:S(2)}) async-start(), calls=%async_computation | async-start | bytes 2097152 | tf_op jit(solution)/shard_map/psum | solution.py:114
  7.8 16.1 %collective-permute-start = (bf16[16,128,256]{2,1,0:T(8,128)(2,1)S(1)}, bf16[16,128,256]{2,1,0:T(8,128)(2,1)S(1)}, u32[]{:S(2)}, u32[]{:S(2)}) collective-permute-start(bf16[16,128,256]{2,1,0:T(8,128)(2,1)S(1)} %get-tuple-element.176), channel_id=1, source_target_pairs={{0,16},{16,0},{32,48},{48,32},{64,80},{80,64},{96,112},{112,96},{1... | collective-permute-start | bytes 3145736 | tf_op jit(solution)/shard_map/ppermute | solution.py:18
  23.9 20.4 %collective-permute-start.1 = (bf16[16,128,256]{2,1,0:T(8,128)(2,1)S(1)}, bf16[16,128,256]{2,1,0:T(8,128)(2,1)S(1)}, u32[]{:S(2)}, u32[]{:S(2)}) collective-permute-start(bf16[16,128,256]{2,1,0:T(8,128)(2,1)S(1)} %get-tuple-element.177), channel_id=1, source_target_pairs={{0,32},{32,0},{16,48},{48,16},{64,96},{96,64},{80,112},{112,80},{1... | collective-permute-start | bytes 3145736 | tf_op jit(solution)/shard_map/ppermute | solution.py:18
  44.3 17.4 %collective-permute-start.2 = (bf16[16,128,256]{2,1,0:T(8,128)(2,1)S(1)}, bf16[16,128,256]{2,1,0:T(8,128)(2,1)S(1)}, u32[]{:S(2)}, u32[]{:S(2)}) collective-permute-start(bf16[16,128,256]{2,1,0:T(8,128)(2,1)S(1)} %get-tuple-element.178), channel_id=1, source_target_pairs={{0,64},{64,0},{16,80},{80,16},{32,96},{96,32},{48,112},{112,48},{1... | collective-permute-start | bytes 3145736 | tf_op jit(solution)/shard_map/ppermute | solution.py:18
  61.6 27.9 %collective-permute-start.3 = (bf16[16,128,256]{2,1,0:T(8,128)(2,1)S(1)}, bf16[16,128,256]{2,1,0:T(8,128)(2,1)S(1)}, u32[]{:S(2)}, u32[]{:S(2)}) collective-permute-start(bf16[16,128,256]{2,1,0:T(8,128)(2,1)S(1)} %get-tuple-element.179), channel_id=1, source_target_pairs={{0,128},{128,0},{16,144},{144,16},{32,160},{160,32},{48,176},{176,... | collective-permute-start | bytes 3145736 | tf_op jit(solution)/shard_map/ppermute | solution.py:18
  89.5 7.6 %copy-start = (bf16[16,128,256]{2,1,0:T(8,128)(2,1)S(1)}, bf16[16,128,256]{2,1,0:T(8,128)(2,1)}, u32[]{:S(2)}) copy-start(bf16[16,128,256]{2,1,0:T(8,128)(2,1)} %param.26) | copy-start | bytes 3145732
  89.5 13.8 %copy-start.2 = (bf16[6,32,256]{2,1,0:T(8,128)(2,1)S(1)}, bf16[6,32,256]{2,1,0:T(8,128)(2,1)}, u32[]{:S(2)}) copy-start(bf16[6,32,256]{2,1,0:T(8,128)(2,1)} %param.33) | copy-start | bytes 294916
  89.5 64.3 %collective-permute-start.4 = (bf16[16,128,256]{2,1,0:T(8,128)(2,1)S(1)}, bf16[16,128,256]{2,1,0:T(8,128)(2,1)}, u32[]{:S(2)}, u32[]{:S(2)}) collective-permute-start(bf16[16,128,256]{2,1,0:T(8,128)(2,1)S(1)} %get-tuple-element.180), channel_id=1, source_target_pairs={{0,256},{256,0},{16,272},{272,16},{32,288},{288,32},{48,304},{304,... | collective-permute-start | bytes 3145736 | tf_op jit(solution)/shard_map/ppermute | solution.py:18
  97.2 33.8 %collective-permute-start.6 = (bf16[8,128,256]{2,1,0:T(8,128)(2,1)S(1)}, bf16[8,128,256]{2,1,0:T(8,128)(2,1)S(1)}, u32[]{:S(2)}, u32[]{:S(2)}) collective-permute-start(bf16[8,128,256]{2,1,0:T(8,128)(2,1)S(1)} %get-tuple-element.175), channel_id=1, source_target_pairs={{16,0},{32,16},{48,32},{64,48},{80,64},{96,80},{112,96},{128,112},... | collective-permute-start | bytes 1572872 | tf_op jit(solution)/shard_map/ppermute | solution.py:29
  98.5 33.3 %collective-permute-start.5 = (bf16[8,128,256]{2,1,0:T(8,128)(2,1)S(1)}, bf16[8,128,256]{2,1,0:T(8,128)(2,1)}, u32[]{:S(2)}, u32[]{:S(2)}) collective-permute-start(bf16[8,128,256]{2,1,0:T(8,128)(2,1)S(1)} %get-tuple-element.174), channel_id=1, source_target_pairs={{0,16},{16,32},{32,48},{48,64},{64,80},{80,96},{96,112},{112,128},... | collective-permute-start | bytes 1572872 | tf_op jit(solution)/shard_map/ppermute | solution.py:26
  131.0 2.6 %copy-start.3 = (f32[16,6,256]{2,0,1:T(8,128)S(1)}, f32[16,6,256]{2,0,1:T(8,128)}, u32[]{:S(2)}) copy-start(f32[16,6,256]{2,0,1:T(8,128)} %param.32) | copy-start | bytes 294916
  131.0 2.6 %copy-start.5 = (s32[16,6]{0,1:T(8,128)S(1)}, s32[16,6]{0,1:T(8,128)}, u32[]{:S(2)}) copy-start(s32[16,6]{0,1:T(8,128)} %param.31) | copy-start | bytes 1156
  131.0 2.6 %copy-start.6 = (s32[16]{0:T(128)S(1)}, s32[16]{0:T(128)}, u32[]{:S(2)}) copy-start(s32[16]{0:T(128)} %param.30) | copy-start | bytes 196
  131.0 0.8 copy-start.1
Sparse Core Ops, SparseCore 0:
  155.3 90.7 all-reduce.1
where the time goes:
time: 256 us
  waiting for transfers between devices  154 us (60%)
  starting transfers between devices  32.1 us (13%)
  blocking collectives  27.7 us (11%)
  other arithmetic  14.8 us (6%)
  between operations  13.5 us (5%)
  local copies, waits for them, and re-layouts  8.28 us (3%)
  matrix products  4.74 us (2%)
    psum x1, waiting for transfers between devices, shards(): lax.psum(section_term.astype(jnp.bfloat16), 'sec').astype(jnp.float32)  90.9 us
    ppermute x5, waiting for transfers between devices, from_partner(): return lax.ppermute(block, axis, route)  63.3 us
    all_gather x1, blocking collectives, shards(): table_piece = lax.all_gather(near_table, 'probe', axis=1, tiled=True)  27.7 us
    ppermute x5, starting transfers between devices, from_partner(): return lax.ppermute(block, axis, route)  26 us
    convert_element_type x1, other arithmetic, build_operand(): (gathered.astype(jnp.float32) * scaling[:, :, None, :]).astype(jnp.bfloat16)  8.86 us
    gather x1, local copies, waits for them, and re-layouts, build_operand(): jnp.take(extended_rows, local_cols.reshape(-1), axis=0)  5.99 us
  transfers between devices with their start and end apart: 8, of which 5 were waited for; matrix products, arithmetic and copies ran while one was open for 9% of the time, Pallas kernels for 0%

commit v1 on v0

v1 whole, which is shorter than its diff:
```python
import functools

import jax
import jax.numpy as jnp
from jax import lax
from jax.experimental import pallas as pl
from jax.experimental.pallas import tpu as pltpu
from jax.sharding import PartitionSpec as P

LOCAL = 4
MAXB = 6
RIM = 8
VMEM_LIMIT = 40 * 1024 * 1024


def vmem():
    return pl.BlockSpec(memory_space=pltpu.VMEM)


def smem():
    return pl.BlockSpec(memory_space=pltpu.SMEM)


def local_kernel(orders, half, weights, gains, out, pairs):
    boxes, cols, width = half.shape
    for level in range(LOCAL):
        source = half if level == 0 else out
        for box in range(boxes):
            block = source[orders[level, box]]
            pairs[box, :, :width] = block
            pairs[box ^ (1 << level), :, width:] = block
        mixed = jnp.dot(
            pairs[...].reshape(boxes * cols, 2 * width),
            weights[level],
            preferred_element_type=jnp.float32,
        ).reshape(boxes, cols, width)
        out[...] = (mixed * gains[level][:, None, :]).astype(out.dtype)


def cross_kernel(levels, rows, weights, out, pairs):
    count, depth, width = rows.shape
    for level in range(levels):
        source = rows if level == 0 else out
        for box in range(count):
            block = source[box]
            pairs[box, :, :width] = block
            pairs[box ^ (1 << level), :, width:] = block
        out[...] = (
            jnp.dot(
                pairs[...].reshape(count * depth, 2 * width),
                weights[level],
                preferred_element_type=jnp.float32,
            )
            .reshape(count, depth, width)
            .astype(out.dtype)
        )


def near_kernel(base, cols_ref, counts, low, own, high, scale, table, out, extended, operand):
    boxes, cols, width = own.shape
    extended[:RIM] = low[...]
    extended[RIM : RIM + boxes] = own[...]
    extended[RIM + boxes :] = high[...]
    first = base[0] - RIM
    for box in range(boxes):
        for slot in range(MAXB):
            block = extended[cols_ref[box, slot] - first].astype(jnp.float32)
            active = (slot < counts[box]).astype(jnp.float32)
            scaled = block * (scale[box, slot : slot + 1, :] * active)
            operand[box, :, slot * width : (slot + 1) * width] = scaled.astype(operand.dtype)
    out[...] = jnp.dot(
        operand[...].reshape(boxes * cols, MAXB * width),
        table[...],
        preferred_element_type=jnp.float32,
    ).reshape(boxes, cols, width)


def params():
    return pltpu.CompilerParams(vmem_limit_bytes=VMEM_LIMIT)


def cost(rows, depth, width, extra):
    return pl.CostEstimate(
        flops=2 * rows * depth * width, bytes_accessed=extra, transcendentals=0
    )


def shards(probes, mixers, box_gains, box_orders, near_count, near_cols, near_scale, near_table):
    boxes, columns, width = probes.shape
    peers = lax.axis_size("bfly")
    levels = mixers.shape[0] - LOCAL
    sec = lax.axis_index("sec")
    me = lax.axis_index("bfly")
    cols = columns // 2
    rows = boxes * cols
    depth = rows // peers
    stacked = mixers.reshape(mixers.shape[0], 2 * width, width)
    half = lax.dynamic_slice_in_dim(probes, sec * cols, cols, axis=1)

    current = pl.pallas_call(
        local_kernel,
        out_shape=jax.ShapeDtypeStruct((boxes, cols, width), jnp.bfloat16),
        in_specs=[smem(), vmem(), vmem(), vmem()],
        out_specs=vmem(),
        scratch_shapes=[pltpu.VMEM((boxes, cols, 2 * width), jnp.bfloat16)],
        compiler_params=params(),
        cost_estimate=cost(LOCAL * rows, 2 * width, width, 4 * rows * width),
        name="local_levels",
    )(box_orders, half, stacked[:LOCAL], box_gains)

    spread = lax.all_to_all(current.reshape(peers, depth, width), "bfly", 0, 0, tiled=True)

    crossed = pl.pallas_call(
        functools.partial(cross_kernel, levels),
        out_shape=jax.ShapeDtypeStruct((peers, depth, width), jnp.bfloat16),
        in_specs=[vmem(), vmem()],
        out_specs=vmem(),
        scratch_shapes=[pltpu.VMEM((peers, depth, 2 * width), jnp.bfloat16)],
        compiler_params=params(),
        cost_estimate=cost(levels * rows, 2 * width, width, 4 * rows * width),
        name="cross_levels",
    )(spread, stacked[LOCAL:])

    far = lax.all_to_all(crossed, "bfly", 0, 0, tiled=True).reshape(boxes, cols, width)

    up = [(i, i + 1) for i in range(peers - 1)]
    down = [(i + 1, i) for i in range(peers - 1)]
    low = lax.ppermute(half[boxes - RIM :], "bfly", up)
    high = lax.ppermute(half[:RIM], "bfly", down)
    table = lax.all_gather(near_table, "probe", axis=1, tiled=True)

    near = pl.pallas_call(
        near_kernel,
        out_shape=jax.ShapeDtypeStruct((boxes, cols, width), jnp.float32),
        in_specs=[smem(), smem(), smem()] + [vmem()] * 5,
        out_specs=vmem(),
        scratch_shapes=[
            pltpu.VMEM((boxes + 2 * RIM, cols, width), jnp.bfloat16),
            pltpu.VMEM((boxes, cols, MAXB * width), jnp.bfloat16),
        ],
        compiler_params=params(),
        cost_estimate=cost(rows, MAXB * width, width, 8 * rows * width),
        name="near_field",
    )(
        (me * boxes)[None],
        near_cols,
        near_count,
        low,
        half,
        high,
        near_scale,
        table.reshape(MAXB * width, width),
    )

    mine = (far.astype(jnp.float32) + near).astype(jnp.bfloat16)
    other = lax.ppermute(mine, "sec", [(0, 1), (1, 0)])
    first = jnp.where(sec == 0, mine, other)
    second = jnp.where(sec == 0, other, mine)
    return jnp.concatenate([first, second], axis=1).astype(jnp.float32)


def solution(mesh):
    return jax.shard_map(
        shards,
        mesh=mesh,
        in_specs=(
            P("bfly", "probe", None),
            P(),
            P(None, "bfly", None),
            P(None, "bfly"),
            P("bfly"),
            P("bfly", None),
            P("bfly", None, None),
            P(None, "probe", None),
        ),
        out_specs=P("bfly", "probe", None),
        check_vma=False,
    )
```

time: 256 us -> 91.2 us (0.36)
  the two profiles are of different devices: /device:TPU:1 before, /device:TPU:31 now
where the time goes in v1:
time: 91.2 us; the launch traced here: 90.8 us
  starting transfers between devices  35 us (38%)
  blocking collectives  27.9 us (31%)
  waiting for transfers between devices  14 us (15%)
  Pallas kernels  8.71 us (10%)
  local copies, waits for them, and re-layouts  3.18 us (3%)
  other arithmetic  1.79 us (2%)
    all_gather x1, blocking collectives, shards(): table = lax.all_gather(near_table, 'probe', axis=1, tiled=True)  27.9 us
    all_to_all x1, waiting for transfers between devices, shards(): lax.all_to_all(current.reshape(peers, depth, width), 'bfly', 0, 0, tiled=...  12.5 us
    ppermute x1, starting transfers between devices, shards(): other = lax.ppermute(mine, 'sec', [(0, 1), (1, 0)])  9.39 us
    all_to_all x1, starting transfers between devices, shards(): lax.all_to_all(current.reshape(peers, depth, width), 'bfly', 0, 0, tiled=...  9.3 us
    all_to_all x1, starting transfers between devices, shards(): lax.all_to_all(crossed, 'bfly', 0, 0, tiled=True)  7.72 us
    ppermute x1, starting transfers between devices, shards(): low = lax.ppermute(half[boxes - RIM:], 'bfly', up)  6.12 us
    pallas_call x1, Pallas kernels, shards(): pl.pallas_call(local_kernel, out_shape=jax.ShapeDtypeStruct((boxes, cols,...  4.04 us
    pallas_call x1, Pallas kernels, shards(): pl.pallas_call(functools.partial(cross_kernel, levels), out_shape=jax.Sha...  2.96 us
  transfers between devices with their start and end apart: 5, of which 2 were waited for; matrix products, arithmetic and copies ran while one was open for 2% of the time, Pallas kernels for 2%

profile of v1, /device:TPU:31, one launch (start us, length us, event | category | flops | bytes accessed | tf_op | source)
XLA Modules:
  0.0 90.8 jit_solution(3982682394813847929)
XLA Ops:
  0.0 0.0 copy-start.3
  0.0 0.0 copy-start.2
  0.0 0.0 copy-start.1
  0.0 1.4 %slice.18 = bf16[4,2,256,256]{3,2,1,0:T(8,128)(2,1)S(1)} slice(bf16[9,2,256,256]{3,2,1,0:T(8,128)(2,1)} %param.9), slice={[0:4], [0:2], [0:256], [0:256]} | slice | bytes 2097152 | tf_op jit(solution)/shard_map/slice | solution.py:109
  1.4 0.1 copy-done.3
  1.6 0.0 copy-done.2
  1.6 0.0 copy-done.1
  1.6 4.0 %local_levels.1 = bf16[16,64,256]{2,1,0:T(8,128)(2,1)} custom-call(s32[4,16]{1,0:T(4,128)S(1)} %copy-done.2, bf16[16,64,256]{2,1,0:T(8,128)(2,1)S(1)} %constant_dynamic-slice_fusion.2.half.own, bf16[4,512,256]{2,1,0:T(8,128)(2,1)S(1)} %bitcast.11, f32[4,16,256]{2,1,0:T(8,128)S(1)} %copy-done.1), custom_call_target="tpu_custom_call" | custom-call | flops 1073741824 | bytes 1048576 | tf_op jit(solution)/shard_map/local_levels/pallas_call | solution.py:100
  5.6 9.3 %all-to-all-start = ((bf16[32,32,256]{2,1,0:T(8,128)(2,1)}), bf16[32,32,256]{2,1,0:T(8,128)(2,1)S(1)}, u32[]{:S(2)}, u32[]{:S(2)}) async-start(bf16[32,32,256]{2,1,0:T(8,128)(2,1)} %bitcast.1), calls=%async_computation | async-start | bytes 1048576 | tf_op jit(solution)/shard_map/all_to_all | solution.py:111
  15.0 1.4 %slice.20 = bf16[5,2,256,256]{3,2,1,0:T(8,128)(2,1)S(1)} slice(bf16[9,2,256,256]{3,2,1,0:T(8,128)(2,1)} %param.9), slice={[4:9], [0:2], [0:256], [0:256]} | slice | bytes 2621440 | tf_op jit(solution)/shard_map/slice | solution.py:122
  16.4 12.5 %all-to-all-done.rows = bf16[32,32,256]{2,1,0:T(8,128)(2,1)S(1)} async-done(((bf16[32,32,256]{2,1,0:T(8,128)(2,1)}), bf16[32,32,256]{2,1,0:T(8,128)(2,1)S(1)}, u32[]{:S(2)}, u32[]{:S(2)}) %all-to-all-start) | async-done | bytes 524320 | tf_op jit(solution)/shard_map/all_to_all | solution.py:111
  28.9 3.0 %cross_levels.1 = bf16[32,32,256]{2,1,0:T(8,128)(2,1)} custom-call(bf16[32,32,256]{2,1,0:T(8,128)(2,1)S(1)} %all-to-all-done.rows, bf16[5,512,256]{2,1,0:T(8,128)(2,1)S(1)} %bitcast.10), custom_call_target="tpu_custom_call" | custom-call | flops 1342177280 | bytes 1048576 | tf_op jit(solution)/shard_map/cross_levels/pallas_call | solution.py:113
  31.8 0.0 copy-start.6
  31.8 0.0 copy-start.4
  31.8 0.0 copy-start.5
  31.8 0.0 copy-start
  31.8 7.7 %all-to-all-start.1 = ((bf16[32,32,256]{2,1,0:T(8,128)(2,1)}), bf16[32,32,256]{2,1,0:T(8,128)(2,1)S(1)}, u32[]{:S(2)}, u32[]{:S(2)}) async-start(bf16[32,32,256]{2,1,0:T(8,128)(2,1)} %cross_levels.1), calls=%async_computation.1 | async-start | bytes 1048576 | tf_op jit(solution)/shard_map/all_to_all | solution.py:124
  39.6 2.5 %collective-permute-start.1 = (bf16[8,64,256]{2,1,0:T(8,128)(2,1)S(1)}, bf16[8,64,256]{2,1,0:T(8,128)(2,1)S(1)}, u32[]{:S(2)}, u32[]{:S(2)}) collective-permute-start(bf16[8,64,256]{2,1,0:T(8,128)(2,1)S(1)} %get-tuple-element.7), channel_id=1, source_target_pairs={{16,0},{32,16},{48,32},{64,48},{80,64},{96,80},{112,96},{128,112},... | collective-permute-start | bytes 786440 | tf_op jit(solution)/shard_map/ppermute | solution.py:129
  42.1 6.1 %collective-permute-start = (bf16[8,64,256]{2,1,0:T(8,128)(2,1)S(1)}, bf16[8,64,256]{2,1,0:T(8,128)(2,1)S(1)}, u32[]{:S(2)}, u32[]{:S(2)}) collective-permute-start(bf16[8,64,256]{2,1,0:T(8,128)(2,1)S(1)} %get-tuple-element.8), channel_id=1, source_target_pairs={{0,16},{16,32},{32,48},{48,64},{64,80},{80,96},{96,112},{112,128},... | collective-permute-start | bytes 786440 | tf_op jit(solution)/shard_map/ppermute | solution.py:128
  48.2 0.0 copy-done.6
  48.2 0.1 copy.9.cols_ref
  48.3 0.0 copy-done.4
  48.3 0.1 copy.10.scale
  48.4 0.0 copy-done.5
  48.4 27.9 %all_gather.3 = bf16[6,256,256]{2,1,0:T(8,128)(2,1)S(1)} all-gather(bf16[6,32,256]{2,1,0:T(8,128)(2,1)S(1)} %copy-done.5), channel_id=1, replica_groups=mesh['bfly'=32,'sec'=2,'probe'=8] {'probe'}, dimensions={1}, use_global_device_ids=true | all-gather | bytes 884736 | tf_op jit(solution)/shard_map/all_gather | solution.py:130
  76.3 0.0 collective-permute-done.1.high
  76.3 0.0 collective-permute-done.low
  76.3 0.0 copy-done
  76.3 1.7 %near_field.1 = f32[16,64,256]{2,1,0:T(8,128)S(1)} custom-call(s32[1]{0:T(128)} %bitcast.4.base, s32[16,6]{1,0:T(8,128)S(1)} %copy.9.cols_ref, s32[16]{0:T(128)S(1)} %copy-done, bf16[8,64,256]{2,1,0:T(8,128)(2,1)S(1)} %collective-permute-done.low, bf16[16,64,256]{2,1,0:T(8,128)(2,1)S(1)} %constant_dynamic-slice_fusion.2.half.own, ...), custom_call_target="tpu_custom_call" | custom-call | flops 805306368 | bytes 2097152 | tf_op jit(solution)/shard_map/near_field/pallas_call | solution.py:132
  78.1 0.0 all-to-all-done.1
  78.1 0.2 fusion
  78.2 9.4 %collective-permute-start.2 = (bf16[16,64,256]{2,1,0:T(8,128)(2,1)S(1)}, bf16[16,64,256]{2,1,0:T(8,128)(2,1)S(1)}, u32[]{:S(2)}, u32[]{:S(2)}) collective-permute-start(bf16[16,64,256]{2,1,0:T(8,128)(2,1)S(1)} %fusion), channel_id=1, source_target_pairs={{0,8},{8,0},{1,9},{9,1},{2,10},{10,2},{3,11},{11,3},{4,12},{12,4},... | collective-permute-start | bytes 1572872 | tf_op jit(solution)/shard_map/ppermute | solution.py:156
  87.6 1.5 %collective-permute-done.2 = bf16[16,64,256]{2,1,0:T(8,128)(2,1)S(1)} collective-permute-done((bf16[16,64,256]{2,1,0:T(8,128)(2,1)S(1)}, bf16[16,64,256]{2,1,0:T(8,128)(2,1)S(1)}, u32[]{:S(2)}, u32[]{:S(2)}) %collective-permute-start.2) | collective-permute-done | bytes 524320 | tf_op jit(solution)/shard_map/ppermute | solution.py:156
  89.2 0.1 broadcast_select_fusion.1
  89.2 1.5 %maximum_convert_fusion = f32[16,128,256]{2,1,0:T(8,128)} fusion(bf16[16,64,256]{2,1,0:T(8,128)(2,1)S(1)} %get-tuple-element.6, bf16[16,64,256]{2,1,0:T(8,128)(2,1)S(1)} %get-tuple-element.5), kind=kLoop, calls=%fused_computation | loop fusion | flops 2097152 | bytes 3145728 | tf_op jit(solution)/shard_map/convert_element_type | solution.py:159
  (2 shorter events, 0.1 us)
Async XLA Ops:
  0.0 1.5 %copy-start.3 = (bf16[16,128,256]{2,1,0:T(8,128)(2,1)S(1)}, bf16[16,128,256]{2,1,0:T(8,128)(2,1)}, u32[]{:S(2)}) copy-start(bf16[16,128,256]{2,1,0:T(8,128)(2,1)} %param.8) | copy-start | bytes 3145732
  0.0 1.6 %copy-start.2 = (s32[4,16]{1,0:T(4,128)S(1)}, s32[4,16]{1,0:T(4,128)}, u32[]{:S(2)}) copy-start(s32[4,16]{1,0:T(4,128)} %orders.1) | copy-start | bytes 772
  0.0 1.6 %copy-start.1 = (f32[4,16,256]{2,1,0:T(8,128)S(1)}, f32[4,16,256]{2,1,0:T(8,128)}, u32[]{:S(2)}) copy-start(f32[4,16,256]{2,1,0:T(8,128)} %gains.1) | copy-start | bytes 196612
  5.6 23.2 %all-to-all-start = ((bf16[32,32,256]{2,1,0:T(8,128)(2,1)}), bf16[32,32,256]{2,1,0:T(8,128)(2,1)S(1)}, u32[]{:S(2)}, u32[]{:S(2)}) async-start(bf16[32,32,256]{2,1,0:T(8,128)(2,1)} %bitcast.1), calls=%async_computation | async-start | bytes 1048576 | tf_op jit(solution)/shard_map/all_to_all | solution.py:111
  31.8 16.4 %copy-start.6 = (s32[16,6]{0,1:T(8,128)S(1)}, s32[16,6]{0,1:T(8,128)}, u32[]{:S(2)}) copy-start(s32[16,6]{0,1:T(8,128)} %param.13) | copy-start | bytes 1156
  31.8 16.5 %copy-start.4 = (f32[16,6,256]{2,0,1:T(8,128)S(1)}, f32[16,6,256]{2,0,1:T(8,128)}, u32[]{:S(2)}) copy-start(f32[16,6,256]{2,0,1:T(8,128)} %param.14) | copy-start | bytes 294916
  31.8 16.6 %copy-start.5 = (bf16[6,32,256]{2,1,0:T(8,128)(2,1)S(1)}, bf16[6,32,256]{2,1,0:T(8,128)(2,1)}, u32[]{:S(2)}) copy-start(bf16[6,32,256]{2,1,0:T(8,128)(2,1)} %param.15) | copy-start | bytes 294916
  31.8 44.5 %copy-start = (s32[16]{0:T(128)S(1)}, s32[16]{0:T(128)}, u32[]{:S(2)}) copy-start(s32[16]{0:T(128)} %counts.1) | copy-start | bytes 196
  31.8 46.2 %all-to-all-start.1 = ((bf16[32,32,256]{2,1,0:T(8,128)(2,1)}), bf16[32,32,256]{2,1,0:T(8,128)(2,1)S(1)}, u32[]{:S(2)}, u32[]{:S(2)}) async-start(bf16[32,32,256]{2,1,0:T(8,128)(2,1)} %cross_levels.1), calls=%async_computation.1 | async-start | bytes 1048576 | tf_op jit(solution)/shard_map/all_to_all | solution.py:124
  39.6 36.7 %collective-permute-start.1 = (bf16[8,64,256]{2,1,0:T(8,128)(2,1)S(1)}, bf16[8,64,256]{2,1,0:T(8,128)(2,1)S(1)}, u32[]{:S(2)}, u32[]{:S(2)}) collective-permute-start(bf16[8,64,256]{2,1,0:T(8,128)(2,1)S(1)} %get-tuple-element.7), channel_id=1, source_target_pairs={{16,0},{32,16},{48,32},{64,48},{80,64},{96,80},{112,96},{128,112},... | collective-permute-start | bytes 786440 | tf_op jit(solution)/shard_map/ppermute | solution.py:129
  42.1 34.2 %collective-permute-start = (bf16[8,64,256]{2,1,0:T(8,128)(2,1)S(1)}, bf16[8,64,256]{2,1,0:T(8,128)(2,1)S(1)}, u32[]{:S(2)}, u32[]{:S(2)}) collective-permute-start(bf16[8,64,256]{2,1,0:T(8,128)(2,1)S(1)} %get-tuple-element.8), channel_id=1, source_target_pairs={{0,16},{16,32},{32,48},{48,64},{64,80},{80,96},{96,112},{112,128},... | collective-permute-start | bytes 786440 | tf_op jit(solution)/shard_map/ppermute | solution.py:128
  78.2 10.9 %collective-permute-start.2 = (bf16[16,64,256]{2,1,0:T(8,128)(2,1)S(1)}, bf16[16,64,256]{2,1,0:T(8,128)(2,1)S(1)}, u32[]{:S(2)}, u32[]{:S(2)}) collective-permute-start(bf16[16,64,256]{2,1,0:T(8,128)(2,1)S(1)} %fusion), channel_id=1, source_target_pairs={{0,8},{8,0},{1,9},{9,1},{2,10},{10,2},{3,11},{11,3},{4,12},{12,4},... | collective-permute-start | bytes 1572872 | tf_op jit(solution)/shard_map/ppermute | solution.py:156

commit v2 on v1

--- a/solution.py
+++ b/solution.py
@@ -70,7 +70,7 @@
             operand[box, :, slot * width : (slot + 1) * width] = scaled.astype(operand.dtype)
     out[...] = jnp.dot(
         operand[...].reshape(boxes * cols, MAXB * width),
-        table[...],
+        table[: MAXB * width],
         preferred_element_type=jnp.float32,
     ).reshape(boxes, cols, width)
 
@@ -96,6 +96,8 @@
     depth = rows // peers
     stacked = mixers.reshape(mixers.shape[0], 2 * width, width)
     half = lax.dynamic_slice_in_dim(probes, sec * cols, cols, axis=1)
+    padded = jnp.concatenate([near_table, near_table[:2]], axis=0)
+    table = lax.all_gather(padded, "probe", axis=1, tiled=True)
 
     current = pl.pallas_call(
         local_kernel,
@@ -110,6 +112,12 @@
 
     spread = lax.all_to_all(current.reshape(peers, depth, width), "bfly", 0, 0, tiled=True)
 
+    up = [(i, i + 1) for i in range(peers - 1)]
+    down = [(i + 1, i) for i in range(peers - 1)]
+    low = lax.ppermute(half[boxes - RIM :], "bfly", up)
+    high = lax.ppermute(half[:RIM], "bfly", down)
+    spread, low, high = lax.optimization_barrier((spread, low, high))
+
     crossed = pl.pallas_call(
         functools.partial(cross_kernel, levels),
         out_shape=jax.ShapeDtypeStruct((peers, depth, width), jnp.bfloat16),
@@ -123,11 +131,6 @@
 
     far = lax.all_to_all(crossed, "bfly", 0, 0, tiled=True).reshape(boxes, cols, width)
 
-    up = [(i, i + 1) for i in range(peers - 1)]
-    down = [(i + 1, i) for i in range(peers - 1)]
-    low = lax.ppermute(half[boxes - RIM :], "bfly", up)
-    high = lax.ppermute(half[:RIM], "bfly", down)
-    table = lax.all_gather(near_table, "probe", axis=1, tiled=True)
 
     near = pl.pallas_call(
         near_kernel,
@@ -149,7 +152,7 @@
         half,
         high,
         near_scale,
-        table.reshape(MAXB * width, width),
+        table.reshape(8 * width, width),
     )
 
     mine = (far.astype(jnp.float32) + near).astype(jnp.bfloat16)

time: 91.2 us -> 88.9 us (0.975)
  the two profiles are of different devices: /device:TPU:31 before, /device:TPU:1 now
where the time goes in v2:
time: 88.9 us; the launch traced here: 88.5 us
  starting transfers between devices  34.3 us (39%)
  waiting for transfers between devices  25 us (28%)
  between operations  13.6 us (15%)
  Pallas kernels  8.71 us (10%)
  local copies, waits for them, and re-layouts  4.42 us (5%)
  other arithmetic  2.44 us (3%)
    all_gather x1, waiting for transfers between devices, shards(): table = lax.all_gather(padded, 'probe', axis=1, tiled=True)  14.7 us
    all_to_all x1, starting transfers between devices, shards(): lax.all_to_all(crossed, 'bfly', 0, 0, tiled=True)  10.6 us
    all_to_all x1, starting transfers between devices, shards(): lax.all_to_all(current.reshape(peers, depth, width), 'bfly', 0, 0, tiled=...  10.5 us
    ppermute x1, starting transfers between devices, shards(): other = lax.ppermute(mine, 'sec', [(0, 1), (1, 0)])  7.93 us
    ppermute x1, waiting for transfers between devices, shards(): high = lax.ppermute(half[:RIM], 'bfly', down)  5.87 us
    pallas_call x1, Pallas kernels, shards(): pl.pallas_call(local_kernel, out_shape=jax.ShapeDtypeStruct((boxes, cols,...  4.04 us
    ppermute x1, starting transfers between devices, shards(): low = lax.ppermute(half[boxes - RIM:], 'bfly', up)  4 us
    pallas_call x1, Pallas kernels, shards(): pl.pallas_call(functools.partial(cross_kernel, levels), out_shape=jax.Sha...  2.96 us
  transfers between devices with their start and end apart: 6, of which 5 were waited for; matrix products, arithmetic and copies ran while one was open for 3% of the time, Pallas kernels for 5%

profile of v2, /device:TPU:1, one launch (start us, length us, event | category | flops | bytes accessed | tf_op | source)
XLA Modules:
  0.0 88.5 jit_solution(6543853830221296557)
XLA Ops:
  6.5 0.0 copy-start.4
  6.5 0.0 copy-start.3
  6.5 0.0 copy-start.2
  6.5 1.4 %slice.21 = bf16[4,2,256,256]{3,2,1,0:T(8,128)(2,1)S(1)} slice(bf16[9,2,256,256]{3,2,1,0:T(8,128)(2,1)} %param.9), slice={[0:4], [0:2], [0:256], [0:256]} | slice | bytes 2097152 | tf_op jit(solution)/shard_map/slice | solution.py:111
  7.9 0.1 copy-done.4
  8.1 0.0 copy-done.3
  8.1 0.0 copy-done.2
  8.1 0.0 copy-start.5
  8.1 0.0 slice-start
  8.2 4.0 %local_levels.1 = bf16[16,64,256]{2,1,0:T(8,128)(2,1)} custom-call(s32[4,16]{1,0:T(4,128)S(1)} %copy-done.3, bf16[16,64,256]{2,1,0:T(8,128)(2,1)S(1)} %constant_dynamic-slice_fusion.2.half.own, bf16[4,512,256]{2,1,0:T(8,128)(2,1)S(1)} %bitcast.11, f32[4,16,256]{2,1,0:T(8,128)S(1)} %copy-done.2), custom_call_target="tpu_custom_call" | custom-call | flops 1073741824 | bytes 1048576 | tf_op jit(solution)/shard_map/local_levels/pallas_call | solution.py:102
  12.2 10.5 %all-to-all-start = ((bf16[32,32,256]{2,1,0:T(8,128)(2,1)}), bf16[32,32,256]{2,1,0:T(8,128)(2,1)S(1)}, u32[]{:S(2)}, u32[]{:S(2)}) async-start(bf16[32,32,256]{2,1,0:T(8,128)(2,1)} %bitcast.1), calls=%async_computation | async-start | bytes 1048576 | tf_op jit(solution)/shard_map/all_to_all | solution.py:113
  22.7 0.0 all-gather.2.cloned.1.call-start
  22.8 0.0 copy-done.5
  22.8 0.0 slice-done
  22.8 0.7 pad_maximum_fusion
  23.4 0.0 all-gather.2.cloned.1.call-update
  23.5 1.3 %collective-permute-start.1 = (bf16[8,64,256]{2,1,0:T(8,128)(2,1)S(1)}, bf16[8,64,256]{2,1,0:T(8,128)(2,1)S(1)}, u32[]{:S(2)}, u32[]{:S(2)}) collective-permute-start(bf16[8,64,256]{2,1,0:T(8,128)(2,1)S(1)} %get-tuple-element.13), channel_id=1, source_target_pairs={{16,0},{32,16},{48,32},{64,48},{80,64},{96,80},{112,96},{128,112},... | collective-permute-start | bytes 786440 | tf_op jit(solution)/shard_map/ppermute | solution.py:118
  24.8 4.0 %collective-permute-start = (bf16[8,64,256]{2,1,0:T(8,128)(2,1)S(1)}, bf16[8,64,256]{2,1,0:T(8,128)(2,1)S(1)}, u32[]{:S(2)}, u32[]{:S(2)}) collective-permute-start(bf16[8,64,256]{2,1,0:T(8,128)(2,1)S(1)} %get-tuple-element.14), channel_id=1, source_target_pairs={{0,16},{16,32},{32,48},{48,64},{64,80},{80,96},{96,112},{112,128},... | collective-permute-start | bytes 786440 | tf_op jit(solution)/shard_map/ppermute | solution.py:117
  28.8 1.4 %slice.25 = bf16[5,2,256,256]{3,2,1,0:T(8,128)(2,1)S(1)} slice(bf16[9,2,256,256]{3,2,1,0:T(8,128)(2,1)} %param.9), slice={[4:9], [0:2], [0:256], [0:256]} | slice | bytes 2621440 | tf_op jit(solution)/shard_map/slice | solution.py:130
  30.2 5.9 %collective-permute-done.1.high = bf16[8,64,256]{2,1,0:T(8,128)(2,1)S(1)} collective-permute-done((bf16[8,64,256]{2,1,0:T(8,128)(2,1)S(1)}, bf16[8,64,256]{2,1,0:T(8,128)(2,1)S(1)}, u32[]{:S(2)}, u32[]{:S(2)}) %collective-permute-start.1) | collective-permute-done | bytes 262176 | tf_op jit(solution)/shard_map/ppermute | solution.py:118
  36.1 0.8 collective-permute-done.low
  36.9 2.0 %all-to-all-done.rows = bf16[32,32,256]{2,1,0:T(8,128)(2,1)S(1)} async-done(((bf16[32,32,256]{2,1,0:T(8,128)(2,1)}), bf16[32,32,256]{2,1,0:T(8,128)(2,1)S(1)}, u32[]{:S(2)}, u32[]{:S(2)}) %all-to-all-start) | async-done | bytes 524320 | tf_op jit(solution)/shard_map/all_to_all | solution.py:113
  39.0 0.0 copy-start.7
  39.0 0.0 copy-start.6
  39.0 0.0 copy-start.1
  39.0 3.0 %cross_levels.1 = bf16[32,32,256]{2,1,0:T(8,128)(2,1)} custom-call(bf16[32,32,256]{2,1,0:T(8,128)(2,1)S(1)} %all-to-all-done.rows, bf16[5,512,256]{2,1,0:T(8,128)(2,1)S(1)} %bitcast.9), custom_call_target="tpu_custom_call" | custom-call | flops 1342177280 | bytes 1048576 | tf_op jit(solution)/shard_map/cross_levels/pallas_call | solution.py:121
  41.9 10.6 %all-to-all-start.1 = ((bf16[32,32,256]{2,1,0:T(8,128)(2,1)}), bf16[32,32,256]{2,1,0:T(8,128)(2,1)S(1)}, u32[]{:S(2)}, u32[]{:S(2)}) async-start(bf16[32,32,256]{2,1,0:T(8,128)(2,1)} %cross_levels.1), calls=%async_computation.1 | async-start | bytes 1048576 | tf_op jit(solution)/shard_map/all_to_all | solution.py:132
  52.5 0.0 copy-done.7
  52.5 0.1 copy.9.cols_ref
  52.6 0.0 copy-done.6
  52.6 0.1 copy.10.scale
  52.7 14.7 %all-gather.2.cloned.1.call-done = bf16[8,256,256]{2,1,0:T(8,128)(2,1)} async-done(((bf16[8,32,256]{2,1,0:T(8,128)(2,1)}), bf16[8,256,256]{2,1,0:T(8,128)(2,1)}) %all-gather.2.cloned.1.call-update) | async-done | bytes 1048592 | tf_op jit(solution)/shard_map/all_gather | solution.py:100
  67.4 0.0 copy-done.1
  67.4 0.0 copy-start
  67.4 1.2 %copy-done = bf16[8,256,256]{2,1,0:T(8,128)(2,1)S(1)} copy-done((bf16[8,256,256]{2,1,0:T(8,128)(2,1)S(1)}, bf16[8,256,256]{2,1,0:T(8,128)(2,1)}, u32[]{:S(2)}) %copy-start) | copy-done | bytes 1048600
  68.7 1.7 %near_field.1 = f32[16,64,256]{2,1,0:T(8,128)S(1)} custom-call(s32[1]{0:T(128)} %bitcast.4.base, s32[16,6]{1,0:T(8,128)S(1)} %copy.9.cols_ref, s32[16]{0:T(128)S(1)} %copy-done.1, bf16[8,64,256]{2,1,0:T(8,128)(2,1)S(1)} %collective-permute-done.low, bf16[16,64,256]{2,1,0:T(8,128)(2,1)S(1)} %constant_dynamic-slice_fusion.2.half.own, ...), custom_call_target="tpu_custom_call" | custom-call | flops 805306368 | bytes 2097152 | tf_op jit(solution)/shard_map/near_field/pallas_call | solution.py:135
  70.4 0.0 all-to-all-done.1
  70.4 0.2 fusion
  70.5 7.9 %collective-permute-start.2 = (bf16[16,64,256]{2,1,0:T(8,128)(2,1)S(1)}, bf16[16,64,256]{2,1,0:T(8,128)(2,1)S(1)}, u32[]{:S(2)}, u32[]{:S(2)}) collective-permute-start(bf16[16,64,256]{2,1,0:T(8,128)(2,1)S(1)} %fusion), channel_id=1, source_target_pairs={{0,8},{8,0},{1,9},{9,1},{2,10},{10,2},{3,11},{11,3},{4,12},{12,4},... | collective-permute-start | bytes 1572872 | tf_op jit(solution)/shard_map/ppermute | solution.py:159
  78.5 1.5 %collective-permute-done.2 = bf16[16,64,256]{2,1,0:T(8,128)(2,1)S(1)} collective-permute-done((bf16[16,64,256]{2,1,0:T(8,128)(2,1)S(1)}, bf16[16,64,256]{2,1,0:T(8,128)(2,1)S(1)}, u32[]{:S(2)}, u32[]{:S(2)}) %collective-permute-start.2) | collective-permute-done | bytes 524320 | tf_op jit(solution)/shard_map/ppermute | solution.py:159
  80.0 0.1 broadcast_select_fusion.1
  80.1 1.5 %maximum_convert_fusion = f32[16,128,256]{2,1,0:T(8,128)} fusion(bf16[16,64,256]{2,1,0:T(8,128)(2,1)S(1)} %get-tuple-element.12, bf16[16,64,256]{2,1,0:T(8,128)(2,1)S(1)} %get-tuple-element.11), kind=kLoop, calls=%fused_computation | loop fusion | flops 2097152 | bytes 3145728 | tf_op jit(solution)/shard_map/convert_element_type | solution.py:162
  (2 shorter events, 0.1 us)
Async XLA Ops:
  6.5 1.5 %copy-start.4 = (bf16[16,128,256]{2,1,0:T(8,128)(2,1)S(1)}, bf16[16,128,256]{2,1,0:T(8,128)(2,1)}, u32[]{:S(2)}) copy-start(bf16[16,128,256]{2,1,0:T(8,128)(2,1)} %param.8) | copy-start | bytes 3145732
  6.5 1.6 %copy-start.3 = (s32[4,16]{1,0:T(4,128)S(1)}, s32[4,16]{1,0:T(4,128)}, u32[]{:S(2)}) copy-start(s32[4,16]{1,0:T(4,128)} %orders.1) | copy-start | bytes 772
  6.5 1.6 %copy-start.2 = (f32[4,16,256]{2,1,0:T(8,128)S(1)}, f32[4,16,256]{2,1,0:T(8,128)}, u32[]{:S(2)}) copy-start(f32[4,16,256]{2,1,0:T(8,128)} %gains.1) | copy-start | bytes 196612
  8.1 14.6 %copy-start.5 = (bf16[6,32,256]{2,1,0:T(8,128)(2,1)S(1)}, bf16[6,32,256]{2,1,0:T(8,128)(2,1)}, u32[]{:S(2)}) copy-start(bf16[6,32,256]{2,1,0:T(8,128)(2,1)} %param.15) | copy-start | bytes 294916
  8.1 14.6 %slice-start = ((bf16[6,32,256]{2,1,0:T(8,128)(2,1)}), bf16[2,32,256]{2,1,0:T(8,128)(2,1)S(1)}, s32[]{:S(2)}) async-start(bf16[6,32,256]{2,1,0:T(8,128)(2,1)} %param.15), calls=%async_computation.3 | async-start | bytes 65536 | tf_op jit(solution)/shard_map/slice | solution.py:99
  12.2 26.8 %all-to-all-start = ((bf16[32,32,256]{2,1,0:T(8,128)(2,1)}), bf16[32,32,256]{2,1,0:T(8,128)(2,1)S(1)}, u32[]{:S(2)}, u32[]{:S(2)}) async-start(bf16[32,32,256]{2,1,0:T(8,128)(2,1)} %bitcast.1), calls=%async_computation | async-start | bytes 1048576 | tf_op jit(solution)/shard_map/all_to_all | solution.py:113
  22.7 44.7 %all-gather.2.cloned.1.call-start = ((), (), s32[]{:S(2)}) async-start(), calls=%async_computation.2 | async-start | bytes 1179648 | tf_op jit(solution)/shard_map/all_gather | solution.py:100
  23.5 12.6 %collective-permute-start.1 = (bf16[8,64,256]{2,1,0:T(8,128)(2,1)S(1)}, bf16[8,64,256]{2,1,0:T(8,128)(2,1)S(1)}, u32[]{:S(2)}, u32[]{:S(2)}) collective-permute-start(bf16[8,64,256]{2,1,0:T(8,128)(2,1)S(1)} %get-tuple-element.13), channel_id=1, source_target_pairs={{16,0},{32,16},{48,32},{64,48},{80,64},{96,80},{112,96},{128,112},... | collective-permute-start | bytes 786440 | tf_op jit(solution)/shard_map/ppermute | solution.py:118
  24.8 12.1 %collective-permute-start = (bf16[8,64,256]{2,1,0:T(8,128)(2,1)S(1)}, bf16[8,64,256]{2,1,0:T(8,128)(2,1)S(1)}, u32[]{:S(2)}, u32[]{:S(2)}) collective-permute-start(bf16[8,64,256]{2,1,0:T(8,128)(2,1)S(1)} %get-tuple-element.14), channel_id=1, source_target_pairs={{0,16},{16,32},{32,48},{48,64},{64,80},{80,96},{96,112},{112,128},... | collective-permute-start | bytes 786440 | tf_op jit(solution)/shard_map/ppermute | solution.py:117
  39.0 13.5 %copy-start.7 = (s32[16,6]{0,1:T(8,128)S(1)}, s32[16,6]{0,1:T(8,128)}, u32[]{:S(2)}) copy-start(s32[16,6]{0,1:T(8,128)} %param.13) | copy-start | bytes 1156
  39.0 13.6 %copy-start.6 = (f32[16,6,256]{2,0,1:T(8,128)S(1)}, f32[16,6,256]{2,0,1:T(8,128)}, u32[]{:S(2)}) copy-start(f32[16,6,256]{2,0,1:T(8,128)} %param.14) | copy-start | bytes 294916
  39.0 28.5 %copy-start.1 = (s32[16]{0:T(128)S(1)}, s32[16]{0:T(128)}, u32[]{:S(2)}) copy-start(s32[16]{0:T(128)} %counts.1) | copy-start | bytes 196
  41.9 28.4 %all-to-all-start.1 = ((bf16[32,32,256]{2,1,0:T(8,128)(2,1)}), bf16[32,32,256]{2,1,0:T(8,128)(2,1)S(1)}, u32[]{:S(2)}, u32[]{:S(2)}) async-start(bf16[32,32,256]{2,1,0:T(8,128)(2,1)} %cross_levels.1), calls=%async_computation.1 | async-start | bytes 1048576 | tf_op jit(solution)/shard_map/all_to_all | solution.py:132
  67.4 1.2 %copy-start = (bf16[8,256,256]{2,1,0:T(8,128)(2,1)S(1)}, bf16[8,256,256]{2,1,0:T(8,128)(2,1)}, u32[]{:S(2)}) copy-start(bf16[8,256,256]{2,1,0:T(8,128)(2,1)} %all-gather.2.cloned.1.call-done) | copy-start | bytes 3145732
  70.5 9.5 %collective-permute-start.2 = (bf16[16,64,256]{2,1,0:T(8,128)(2,1)S(1)}, bf16[16,64,256]{2,1,0:T(8,128)(2,1)S(1)}, u32[]{:S(2)}, u32[]{:S(2)}) collective-permute-start(bf16[16,64,256]{2,1,0:T(8,128)(2,1)S(1)} %fusion), channel_id=1, source_target_pairs={{0,8},{8,0},{1,9},{9,1},{2,10},{10,2},{3,11},{11,3},{4,12},{12,4},... | collective-permute-start | bytes 1572872 | tf_op jit(solution)/shard_map/ppermute | solution.py:159
Sparse Core Ops, SparseCore 0:
  25.6 41.7 all-gather.1

commit v3 on v2

--- a/solution.py
+++ b/solution.py
@@ -17,18 +17,33 @@
     return pl.BlockSpec(memory_space=pltpu.VMEM)
 
 
+def hbm():
+    return pl.BlockSpec(memory_space=pltpu.HBM)
+
+
 def smem():
     return pl.BlockSpec(memory_space=pltpu.SMEM)
 
 
-def local_kernel(orders, half, weights, gains, out, pairs):
-    boxes, cols, width = half.shape
+def local_kernel(orders, which, probes, mixers, gains, out, half, weights, pairs, half_sem, sems):
+    boxes, cols, width = out.shape
+    columns = pl.ds(pl.multiple_of(which[0] * cols, cols), cols)
+    fetch = pltpu.make_async_copy(probes.at[:, columns, :], half, half_sem)
+    fetch.start()
+    loads = [
+        pltpu.make_async_copy(mixers.at[level], weights.at[level], sems.at[level])
+        for level in range(LOCAL)
+    ]
+    for load in loads:
+        load.start()
+    fetch.wait()
     for level in range(LOCAL):
         source = half if level == 0 else out
         for box in range(boxes):
             block = source[orders[level, box]]
             pairs[box, :, :width] = block
             pairs[box ^ (1 << level), :, width:] = block
+        loads[level].wait()
         mixed = jnp.dot(
             pairs[...].reshape(boxes * cols, 2 * width),
             weights[level],
@@ -56,8 +71,14 @@
         )
 
 
-def near_kernel(base, cols_ref, counts, low, own, high, scale, table, out, extended, operand):
+def near_kernel(base, cols_ref, counts, low, own, high, scale, mine, other, out, extended, operand, table):
     boxes, cols, width = own.shape
+    parts, slots, depth, _ = mine.shape
+    for block, start in ((mine, base[1]), (other, base[2])):
+        for part in range(parts):
+            for slot in range(slots):
+                at = pl.multiple_of(start + base[3 + part] + slot * width, depth)
+                table[pl.ds(at, depth), :] = block[part, slot]
     extended[:RIM] = low[...]
     extended[RIM : RIM + boxes] = own[...]
     extended[RIM + boxes :] = high[...]
@@ -70,9 +91,13 @@
             operand[box, :, slot * width : (slot + 1) * width] = scaled.astype(operand.dtype)
     out[...] = jnp.dot(
         operand[...].reshape(boxes * cols, MAXB * width),
-        table[: MAXB * width],
+        table[...],
         preferred_element_type=jnp.float32,
     ).reshape(boxes, cols, width)
+
+
+def in_hbm(array):
+    return pltpu.with_memory_space_constraint(array, pltpu.HBM)
 
 
 def params():
@@ -95,32 +120,48 @@
     rows = boxes * cols
     depth = rows // peers
     stacked = mixers.reshape(mixers.shape[0], 2 * width, width)
-    half = lax.dynamic_slice_in_dim(probes, sec * cols, cols, axis=1)
-    padded = jnp.concatenate([near_table, near_table[:2]], axis=0)
-    table = lax.all_gather(padded, "probe", axis=1, tiled=True)
-
     current = pl.pallas_call(
         local_kernel,
-        out_shape=jax.ShapeDtypeStruct((boxes, cols, width), jnp.bfloat16),
-        in_specs=[smem(), vmem(), vmem(), vmem()],
+        out_shape=pltpu.HBM((boxes, cols, width), jnp.bfloat16),
+        in_specs=[smem(), smem(), hbm(), hbm(), vmem()],
         out_specs=vmem(),
-        scratch_shapes=[pltpu.VMEM((boxes, cols, 2 * width), jnp.bfloat16)],
+        scratch_shapes=[
+            pltpu.VMEM((boxes, cols, width), jnp.bfloat16),
+            pltpu.VMEM((LOCAL, 2 * width, width), jnp.bfloat16),
+            pltpu.VMEM((boxes, cols, 2 * width), jnp.bfloat16),
+            pltpu.SemaphoreType.DMA,
+            pltpu.SemaphoreType.DMA((LOCAL,)),
+        ],
         compiler_params=params(),
         cost_estimate=cost(LOCAL * rows, 2 * width, width, 4 * rows * width),
         name="local_levels",
-    )(box_orders, half, stacked[:LOCAL], box_gains)
+    )(box_orders, sec[None], in_hbm(probes), in_hbm(stacked), box_gains)
 
     spread = lax.all_to_all(current.reshape(peers, depth, width), "bfly", 0, 0, tiled=True)
 
+    half = lax.dynamic_slice_in_dim(probes, sec * cols, cols, axis=1)
     up = [(i, i + 1) for i in range(peers - 1)]
     down = [(i + 1, i) for i in range(peers - 1)]
     low = lax.ppermute(half[boxes - RIM :], "bfly", up)
     high = lax.ppermute(half[:RIM], "bfly", down)
-    spread, low, high = lax.optimization_barrier((spread, low, high))
+
+    slots = MAXB // 2
+    splits = lax.axis_size("probe")
+    here = lax.axis_index("probe")
+    table = lax.dynamic_slice_in_dim(near_table, sec * slots, slots, axis=0)[None]
+    placed, step = [0], splits // 2
+    while step:
+        if step == 1:
+            spread, low, high, table = lax.optimization_barrier((spread, low, high, table))
+        got = lax.ppermute(table, "probe", [(i, i ^ step) for i in range(splits)])
+        table = jnp.concatenate([table, got], axis=0)
+        placed += [i ^ step for i in placed]
+        step //= 2
+    other_table = lax.ppermute(table, "sec", [(0, 1), (1, 0)])
 
     crossed = pl.pallas_call(
         functools.partial(cross_kernel, levels),
-        out_shape=jax.ShapeDtypeStruct((peers, depth, width), jnp.bfloat16),
+        out_shape=pltpu.HBM((peers, depth, width), jnp.bfloat16),
         in_specs=[vmem(), vmem()],
         out_specs=vmem(),
         scratch_shapes=[pltpu.VMEM((peers, depth, 2 * width), jnp.bfloat16)],
@@ -131,29 +172,24 @@
 
     far = lax.all_to_all(crossed, "bfly", 0, 0, tiled=True).reshape(boxes, cols, width)
 
-
+    base = jnp.stack(
+        [me * boxes, sec * (slots * width), (1 - sec) * (slots * width)]
+        + [(here ^ i) * near_table.shape[1] for i in placed]
+    )
     near = pl.pallas_call(
         near_kernel,
         out_shape=jax.ShapeDtypeStruct((boxes, cols, width), jnp.float32),
-        in_specs=[smem(), smem(), smem()] + [vmem()] * 5,
+        in_specs=[smem(), smem(), smem()] + [vmem()] * 6,
         out_specs=vmem(),
         scratch_shapes=[
             pltpu.VMEM((boxes + 2 * RIM, cols, width), jnp.bfloat16),
             pltpu.VMEM((boxes, cols, MAXB * width), jnp.bfloat16),
+            pltpu.VMEM((MAXB * width, width), jnp.bfloat16),
         ],
         compiler_params=params(),
         cost_estimate=cost(rows, MAXB * width, width, 8 * rows * width),
         name="near_field",
-    )(
-        (me * boxes)[None],
-        near_cols,
-        near_count,
-        low,
-        half,
-        high,
-        near_scale,
-        table.reshape(8 * width, width),
-    )
+    )(base, near_cols, near_count, low, half, high, near_scale, table, other_table)
 
     mine = (far.astype(jnp.float32) + near).astype(jnp.bfloat16)
     other = lax.ppermute(mine, "sec", [(0, 1), (1, 0)])

time: 88.9 us -> 80.1 us (0.901)
  starting transfers between devices: 34.3 us -> 55.3 us
  waiting for transfers between devices: 25 us -> 8.39 us
  between operations: 13.6 us -> 0.28 us
  Pallas kernels: 8.71 us -> 10.3 us
  local copies, waits for them, and re-layouts: 4.42 us -> 3.36 us
    ppermute x0 -> x4, starting transfers between devices: none -> 23.6 us  [the longest x3 17 us: shards(): got = lax.ppermute(table, 'probe', [(i, i ^ step) for i in range(splits)])]
    all_gather x1 -> x0, waiting for transfers between devices: 14.7 us -> none  [shards(): table = lax.all_gather(padded, 'probe', axis=1, tiled=True)]
    ppermute x0 -> x4, waiting for transfers between devices: none -> 6.87 us  [the longest x3 5.89 us: shards(): got = lax.ppermute(table, 'probe', [(i, i ^ step) for i in range(splits)])]
    ppermute x1, waiting for transfers between devices: 5.87 us -> 0.01 us  [shards(): high = lax.ppermute(half[:RIM], 'bfly', down)]
    ppermute x1, starting transfers between devices: 7.93 us -> 4.78 us  [shards(): other = lax.ppermute(mine, 'sec', [(0, 1), (1, 0)])]
    all_to_all x1, waiting for transfers between devices: 2.05 us -> 0.01 us  [shards(): lax.all_to_all(current.reshape(peers, depth, width), 'bfly', 0, 0, tiled=...]
    pallas_call x2, Pallas kernels: 7 us -> 8.54 us  [the longest x1 5.58 us: shards(): pl.pallas_call(local_kernel, out_shape=pltpu.HBM((boxes, cols, width), jn...]
    slice x3 -> x0, local copies, waits for them, and re-layouts: 1.39 us -> none  [the longest x1 1.38 us: shards(): stacked[:LOCAL]]
  transfers between devices with their start and end apart: 6 -> 9, of which waited for: 5 -> 4; matrix products, arithmetic and copies ran while one was open for 3% -> 2% of each run, Pallas kernels for 5% -> 2%
where the time goes in v3:
time: 80.1 us; the launch traced here: 79.5 us
  starting transfers between devices  55.3 us (69%)
  Pallas kernels  10.3 us (13%)
  waiting for transfers between devices  8.39 us (10%)
  local copies, waits for them, and re-layouts  3.36 us (4%)
  other arithmetic  1.83 us (2%)
    ppermute x3, starting transfers between devices, shards(): got = lax.ppermute(table, 'probe', [(i, i ^ step) for i in range(splits)])  17 us
    all_to_all x1, starting transfers between devices, shards(): lax.all_to_all(crossed, 'bfly', 0, 0, tiled=True)  11.2 us
    all_to_all x1, starting transfers between devices, shards(): lax.all_to_all(current.reshape(peers, depth, width), 'bfly', 0, 0, tiled=...  10.5 us
    ppermute x1, starting transfers between devices, shards(): other_table = lax.ppermute(table, 'sec', [(0, 1), (1, 0)])  6.56 us
    ppermute x3, waiting for transfers between devices, shards(): got = lax.ppermute(table, 'probe', [(i, i ^ step) for i in range(splits)])  5.89 us
    pallas_call x1, Pallas kernels, shards(): pl.pallas_call(local_kernel, out_shape=pltpu.HBM((boxes, cols, width), jn...  5.58 us
    ppermute x1, starting transfers between devices, shards(): other = lax.ppermute(mine, 'sec', [(0, 1), (1, 0)])  4.78 us
    ppermute x1, starting transfers between devices, shards(): low = lax.ppermute(half[boxes - RIM:], 'bfly', up)  4 us
  transfers between devices with their start and end apart: 9, of which 4 were waited for; matrix products, arithmetic and copies ran while one was open for 2% of the time, Pallas kernels for 2%

profile of v3, /device:TPU:1, one launch (start us, length us, event | category | flops | bytes accessed | tf_op | source)
XLA Modules:
  0.0 79.5 jit_solution(13056833343049348473)
XLA Ops:
  0.0 0.0 copy-start
  0.0 0.0 copy-start.1
  0.0 0.9 %copy-done.1 = f32[4,16,256]{2,1,0:T(8,128)S(1)} copy-done((f32[4,16,256]{2,1,0:T(8,128)S(1)}, f32[4,16,256]{2,1,0:T(8,128)}, u32[]{:S(2)}) %copy-start.1) | copy-done | bytes 65560
  0.9 0.0 copy-start.2
  0.9 0.7 copy-done.2
  1.6 0.0 copy-start.4
  1.6 5.6 %local_levels.1 = bf16[16,64,256]{2,1,0:T(8,128)(2,1)} custom-call(s32[4,16]{1,0:T(4,128)S(1)} %copy-done.2, s32[1]{0:T(128)} %bitcast.which, bf16[16,128,256]{2,1,0:T(8,128)(2,1)} %probes.1, bf16[9,512,256]{2,1,0:T(8,128)(2,1)} %bitcast.22, f32[4,16,256]{2,1,0:T(8,128)S(1)} %copy-done.1), custom_call_target="tpu_custom_call" | custom-call | flops 1073741824 | bytes 1048576 | tf_op jit(solution)/shard_map/local_levels/pallas_call | solution.py:123
  7.2 10.5 %all-to-all-start = ((bf16[32,32,256]{2,1,0:T(8,128)(2,1)}), bf16[32,32,256]{2,1,0:T(8,128)(2,1)S(1)}, u32[]{:S(2)}, u32[]{:S(2)}) async-start(bf16[32,32,256]{2,1,0:T(8,128)(2,1)} %bitcast.24), calls=%async_computation | async-start | bytes 1048576 | tf_op jit(solution)/shard_map/all_to_all | solution.py:140
  17.7 0.0 copy-done
  17.7 10.6 %collective-permute-start.2 = (bf16[1,3,32,256]{3,2,1,0:T(8,128)(2,1)S(1)}, bf16[1,3,32,256]{3,2,1,0:T(8,128)(2,1)S(1)}, u32[]{:S(2)}, u32[]{:S(2)}) collective-permute-start(bf16[1,3,32,256]{3,2,1,0:T(8,128)(2,1)S(1)} %dynamic-slice_bitcast_fusion), channel_id=1, source_target_pairs={{0,4},{1,5},{2,6},{3,7},{4,0},{5,1},{6,2},{7,3},{8,12},{9,13},{10,... | collective-permute-start | bytes 147464 | tf_op jit(solution)/shard_map/ppermute | solution.py:156
  28.4 0.0 copy-done.4
  28.4 1.3 %collective-permute-start.1 = (bf16[8,64,256]{2,1,0:T(8,128)(2,1)S(1)}, bf16[8,64,256]{2,1,0:T(8,128)(2,1)S(1)}, u32[]{:S(2)}, u32[]{:S(2)}) collective-permute-start(bf16[8,64,256]{2,1,0:T(8,128)(2,1)S(1)} %get-tuple-element.15), channel_id=1, source_target_pairs={{16,0},{32,16},{48,32},{64,48},{80,64},{96,80},{112,96},{128,112},... | collective-permute-start | bytes 786440 | tf_op jit(solution)/shard_map/ppermute | solution.py:146
  29.7 4.0 %collective-permute-start = (bf16[8,64,256]{2,1,0:T(8,128)(2,1)S(1)}, bf16[8,64,256]{2,1,0:T(8,128)(2,1)S(1)}, u32[]{:S(2)}, u32[]{:S(2)}) collective-permute-start(bf16[8,64,256]{2,1,0:T(8,128)(2,1)S(1)} %get-tuple-element.16), channel_id=1, source_target_pairs={{0,16},{16,32},{32,48},{48,64},{64,80},{80,96},{96,112},{112,128},... | collective-permute-start | bytes 786440 | tf_op jit(solution)/shard_map/ppermute | solution.py:145
  33.7 0.0 collective-permute-done.2
  33.8 4.0 %collective-permute-start.3 = (bf16[2,3,32,256]{3,2,1,0:T(8,128)(2,1)S(1)}, bf16[2,3,32,256]{3,2,1,0:T(8,128)(2,1)S(1)}, u32[]{:S(2)}, u32[]{:S(2)}) collective-permute-start(bf16[2,3,32,256]{3,2,1,0:T(8,128)(2,1)S(1)} %pad_maximum_fusion.1), channel_id=1, source_target_pairs={{0,2},{1,3},{2,0},{3,1},{4,6},{5,7},{6,4},{7,5},{8,10},{9,11},{10,... | collective-permute-start | bytes 294920 | tf_op jit(solution)/shard_map/ppermute | solution.py:156
  37.8 1.4 %slice.14 = bf16[5,2,256,256]{3,2,1,0:T(8,128)(2,1)S(1)} slice(bf16[9,2,256,256]{3,2,1,0:T(8,128)(2,1)} %param.9), slice={[4:9], [0:2], [0:256], [0:256]} | slice | bytes 2621440 | tf_op jit(solution)/shard_map/slice | solution.py:171
  39.2 1.9 %collective-permute-done.3 = bf16[2,3,32,256]{3,2,1,0:T(8,128)(2,1)S(1)} collective-permute-done((bf16[2,3,32,256]{3,2,1,0:T(8,128)(2,1)S(1)}, bf16[2,3,32,256]{3,2,1,0:T(8,128)(2,1)S(1)}, u32[]{:S(2)}, u32[]{:S(2)}) %collective-permute-start.3) | collective-permute-done | bytes 98336 | tf_op jit(solution)/shard_map/ppermute | solution.py:156
  41.1 0.0 collective-permute-done.1.high
  41.1 0.0 collective-permute-done.low
  41.1 0.0 all-to-all-done.rows
  41.1 0.0 copy-start.7
  41.1 0.0 copy-start.6
  41.1 3.0 %cross_levels.1 = bf16[32,32,256]{2,1,0:T(8,128)(2,1)} custom-call(bf16[32,32,256]{2,1,0:T(8,128)(2,1)S(1)} %all-to-all-done.rows, bf16[5,512,256]{2,1,0:T(8,128)(2,1)S(1)} %bitcast.21), custom_call_target="tpu_custom_call" | custom-call | flops 1342177280 | bytes 1048576 | tf_op jit(solution)/shard_map/cross_levels/pallas_call | solution.py:162
  44.1 0.0 copy-start.5
  44.1 0.0 copy-start.3
  44.1 11.2 %all-to-all-start.1 = ((bf16[32,32,256]{2,1,0:T(8,128)(2,1)}), bf16[32,32,256]{2,1,0:T(8,128)(2,1)S(1)}, u32[]{:S(2)}, u32[]{:S(2)}) async-start(bf16[32,32,256]{2,1,0:T(8,128)(2,1)} %cross_levels.1), calls=%async_computation.1 | async-start | bytes 1048576 | tf_op jit(solution)/shard_map/all_to_all | solution.py:173
  55.3 2.4 %collective-permute-start.4 = (bf16[4,3,32,256]{3,2,1,0:T(8,128)(2,1)S(1)}, bf16[4,3,32,256]{3,2,1,0:T(8,128)(2,1)S(1)}, u32[]{:S(2)}, u32[]{:S(2)}) collective-permute-start(bf16[4,3,32,256]{3,2,1,0:T(8,128)(2,1)S(1)} %pad_maximum_fusion), channel_id=1, source_target_pairs={{0,1},{1,0},{2,3},{3,2},{4,5},{5,4},{6,7},{7,6},{8,9},{9,8},{10,11... | collective-permute-start | bytes 589832 | tf_op jit(solution)/shard_map/ppermute | solution.py:156
  57.7 4.0 %collective-permute-done.4 = bf16[4,3,32,256]{3,2,1,0:T(8,128)(2,1)S(1)} collective-permute-done((bf16[4,3,32,256]{3,2,1,0:T(8,128)(2,1)S(1)}, bf16[4,3,32,256]{3,2,1,0:T(8,128)(2,1)S(1)}, u32[]{:S(2)}, u32[]{:S(2)}) %collective-permute-start.4) | collective-permute-done | bytes 196640 | tf_op jit(solution)/shard_map/ppermute | solution.py:156
  61.7 6.6 %collective-permute-start.5 = (bf16[8,3,32,256]{3,2,1,0:T(8,128)(2,1)S(1)}, bf16[8,3,32,256]{3,2,1,0:T(8,128)(2,1)S(1)}, u32[]{:S(2)}, u32[]{:S(2)}) collective-permute-start(bf16[8,3,32,256]{3,2,1,0:T(8,128)(2,1)S(1)} %constant_dynamic-update-slice_fusion.mine), channel_id=1, source_target_pairs={{0,8},{8,0},{1,9},{9,1},{2,10},{10,2},{3,11},{11,3},{4,12},{12,4},... | collective-permute-start | bytes 1179656 | tf_op jit(solution)/shard_map/ppermute | solution.py:160
  68.3 0.0 copy-done.7
  68.3 0.1 copy.9.cols_ref
  68.4 0.0 copy-done.6
  68.4 0.1 copy.10.scale
  68.5 0.1 stack.47.base
  68.6 0.0 copy-done.5
  68.6 0.1 constant_dynamic-slice_fusion.2.own
  68.6 1.0 %collective-permute-done.5.other = bf16[8,3,32,256]{3,2,1,0:T(8,128)(2,1)S(1)} collective-permute-done((bf16[8,3,32,256]{3,2,1,0:T(8,128)(2,1)S(1)}, bf16[8,3,32,256]{3,2,1,0:T(8,128)(2,1)S(1)}, u32[]{:S(2)}, u32[]{:S(2)}) %collective-permute-start.5) | collective-permute-done | bytes 393248 | tf_op jit(solution)/shard_map/ppermute | solution.py:160
  69.6 0.0 copy-done.3
  69.6 1.8 %near_field.1 = f32[16,64,256]{2,1,0:T(8,128)S(1)} custom-call(s32[11]{0:T(128)S(1)} %stack.47.base, s32[16,6]{1,0:T(8,128)S(1)} %copy.9.cols_ref, s32[16]{0:T(128)S(1)} %copy-done.3, bf16[8,64,256]{2,1,0:T(8,128)(2,1)S(1)} %collective-permute-done.low, bf16[16,64,256]{2,1,0:T(8,128)(2,1)S(1)} %constant_dynamic-slice_fusion.2.own, ...), custom_call_target="tpu_custom_call" | custom-call | flops 805306368 | bytes 2097152 | tf_op jit(solution)/shard_map/near_field/pallas_call | solution.py:179
  71.4 0.0 all-to-all-done.1
  71.4 0.2 fusion
  71.6 4.8 %collective-permute-start.6 = (bf16[16,64,256]{2,1,0:T(8,128)(2,1)S(1)}, bf16[16,64,256]{2,1,0:T(8,128)(2,1)S(1)}, u32[]{:S(2)}, u32[]{:S(2)}) collective-permute-start(bf16[16,64,256]{2,1,0:T(8,128)(2,1)S(1)} %fusion), channel_id=1, source_target_pairs={{0,8},{8,0},{1,9},{9,1},{2,10},{10,2},{3,11},{11,3},{4,12},{12,4},... | collective-permute-start | bytes 1572872 | tf_op jit(solution)/shard_map/ppermute | solution.py:195
  76.4 1.5 %collective-permute-done.6 = bf16[16,64,256]{2,1,0:T(8,128)(2,1)S(1)} collective-permute-done((bf16[16,64,256]{2,1,0:T(8,128)(2,1)S(1)}, bf16[16,64,256]{2,1,0:T(8,128)(2,1)S(1)}, u32[]{:S(2)}, u32[]{:S(2)}) %collective-permute-start.6) | collective-permute-done | bytes 524320 | tf_op jit(solution)/shard_map/ppermute | solution.py:195
  77.9 0.1 broadcast_select_fusion.1
  77.9 1.5 %maximum_convert_fusion = f32[16,128,256]{2,1,0:T(8,128)} fusion(bf16[16,64,256]{2,1,0:T(8,128)(2,1)S(1)} %get-tuple-element.14, bf16[16,64,256]{2,1,0:T(8,128)(2,1)S(1)} %get-tuple-element.13), kind=kLoop, calls=%fused_computation | loop fusion | flops 2097152 | bytes 3145728 | tf_op jit(solution)/shard_map/convert_element_type | solution.py:198
  (6 shorter events, 0.1 us)
Async XLA Ops:
  0.0 17.7 %copy-start = (bf16[6,32,256]{2,1,0:T(8,128)(2,1)S(1)}, bf16[6,32,256]{2,1,0:T(8,128)(2,1)}, u32[]{:S(2)}) copy-start(bf16[6,32,256]{2,1,0:T(8,128)(2,1)} %param.15) | copy-start | bytes 294916
  0.0 0.9 %copy-start.1 = (f32[4,16,256]{2,1,0:T(8,128)S(1)}, f32[4,16,256]{2,1,0:T(8,128)}, u32[]{:S(2)}) copy-start(f32[4,16,256]{2,1,0:T(8,128)} %gains.1) | copy-start | bytes 196612
  0.9 0.7 copy-start.2
  1.6 26.8 %copy-start.4 = (bf16[16,128,256]{2,1,0:T(8,128)(2,1)S(1)}, bf16[16,128,256]{2,1,0:T(8,128)(2,1)}, u32[]{:S(2)}) copy-start(bf16[16,128,256]{2,1,0:T(8,128)(2,1)} %probes.1) | copy-start | bytes 3145732
  7.2 34.0 %all-to-all-start = ((bf16[32,32,256]{2,1,0:T(8,128)(2,1)}), bf16[32,32,256]{2,1,0:T(8,128)(2,1)S(1)}, u32[]{:S(2)}, u32[]{:S(2)}) async-start(bf16[32,32,256]{2,1,0:T(8,128)(2,1)} %bitcast.24), calls=%async_computation | async-start | bytes 1048576 | tf_op jit(solution)/shard_map/all_to_all | solution.py:140
  17.7 16.0 %collective-permute-start.2 = (bf16[1,3,32,256]{3,2,1,0:T(8,128)(2,1)S(1)}, bf16[1,3,32,256]{3,2,1,0:T(8,128)(2,1)S(1)}, u32[]{:S(2)}, u32[]{:S(2)}) collective-permute-start(bf16[1,3,32,256]{3,2,1,0:T(8,128)(2,1)S(1)} %dynamic-slice_bitcast_fusion), channel_id=1, source_target_pairs={{0,4},{1,5},{2,6},{3,7},{4,0},{5,1},{6,2},{7,3},{8,12},{9,13},{10,... | collective-permute-start | bytes 147464 | tf_op jit(solution)/shard_map/ppermute | solution.py:156
  28.4 12.7 %collective-permute-start.1 = (bf16[8,64,256]{2,1,0:T(8,128)(2,1)S(1)}, bf16[8,64,256]{2,1,0:T(8,128)(2,1)S(1)}, u32[]{:S(2)}, u32[]{:S(2)}) collective-permute-start(bf16[8,64,256]{2,1,0:T(8,128)(2,1)S(1)} %get-tuple-element.15), channel_id=1, source_target_pairs={{16,0},{32,16},{48,32},{64,48},{80,64},{96,80},{112,96},{128,112},... | collective-permute-start | bytes 786440 | tf_op jit(solution)/shard_map/ppermute | solution.py:146
  29.7 11.4 %collective-permute-start = (bf16[8,64,256]{2,1,0:T(8,128)(2,1)S(1)}, bf16[8,64,256]{2,1,0:T(8,128)(2,1)S(1)}, u32[]{:S(2)}, u32[]{:S(2)}) collective-permute-start(bf16[8,64,256]{2,1,0:T(8,128)(2,1)S(1)} %get-tuple-element.16), channel_id=1, source_target_pairs={{0,16},{16,32},{32,48},{48,64},{64,80},{80,96},{96,112},{112,128},... | collective-permute-start | bytes 786440 | tf_op jit(solution)/shard_map/ppermute | solution.py:145
  33.8 7.3 %collective-permute-start.3 = (bf16[2,3,32,256]{3,2,1,0:T(8,128)(2,1)S(1)}, bf16[2,3,32,256]{3,2,1,0:T(8,128)(2,1)S(1)}, u32[]{:S(2)}, u32[]{:S(2)}) collective-permute-start(bf16[2,3,32,256]{3,2,1,0:T(8,128)(2,1)S(1)} %pad_maximum_fusion.1), channel_id=1, source_target_pairs={{0,2},{1,3},{2,0},{3,1},{4,6},{5,7},{6,4},{7,5},{8,10},{9,11},{10,... | collective-permute-start | bytes 294920 | tf_op jit(solution)/shard_map/ppermute | solution.py:156
  41.1 27.2 %copy-start.7 = (s32[16,6]{0,1:T(8,128)S(1)}, s32[16,6]{0,1:T(8,128)}, u32[]{:S(2)}) copy-start(s32[16,6]{0,1:T(8,128)} %param.13) | copy-start | bytes 1156
  41.1 27.3 %copy-start.6 = (f32[16,6,256]{2,0,1:T(8,128)S(1)}, f32[16,6,256]{2,0,1:T(8,128)}, u32[]{:S(2)}) copy-start(f32[16,6,256]{2,0,1:T(8,128)} %param.14) | copy-start | bytes 294916
  44.1 24.4 %copy-start.5 = (bf16[16,128,256]{2,1,0:T(8,128)(2,1)S(1)}, bf16[16,128,256]{2,1,0:T(8,128)(2,1)}, u32[]{:S(2)}) copy-start(bf16[16,128,256]{2,1,0:T(8,128)(2,1)} %probes.1) | copy-start | bytes 3145732
  44.1 25.5 %copy-start.3 = (s32[16]{0:T(128)S(1)}, s32[16]{0:T(128)}, u32[]{:S(2)}) copy-start(s32[16]{0:T(128)} %counts.1) | copy-start | bytes 196
  44.1 27.3 %all-to-all-start.1 = ((bf16[32,32,256]{2,1,0:T(8,128)(2,1)}), bf16[32,32,256]{2,1,0:T(8,128)(2,1)S(1)}, u32[]{:S(2)}, u32[]{:S(2)}) async-start(bf16[32,32,256]{2,1,0:T(8,128)(2,1)} %cross_levels.1), calls=%async_computation.1 | async-start | bytes 1048576 | tf_op jit(solution)/shard_map/all_to_all | solution.py:173
  55.3 6.4 %collective-permute-start.4 = (bf16[4,3,32,256]{3,2,1,0:T(8,128)(2,1)S(1)}, bf16[4,3,32,256]{3,2,1,0:T(8,128)(2,1)S(1)}, u32[]{:S(2)}, u32[]{:S(2)}) collective-permute-start(bf16[4,3,32,256]{3,2,1,0:T(8,128)(2,1)S(1)} %pad_maximum_fusion), channel_id=1, source_target_pairs={{0,1},{1,0},{2,3},{3,2},{4,5},{5,4},{6,7},{7,6},{8,9},{9,8},{10,11... | collective-permute-start | bytes 589832 | tf_op jit(solution)/shard_map/ppermute | solution.py:156
  61.7 7.9 %collective-permute-start.5 = (bf16[8,3,32,256]{3,2,1,0:T(8,128)(2,1)S(1)}, bf16[8,3,32,256]{3,2,1,0:T(8,128)(2,1)S(1)}, u32[]{:S(2)}, u32[]{:S(2)}) collective-permute-start(bf16[8,3,32,256]{3,2,1,0:T(8,128)(2,1)S(1)} %constant_dynamic-update-slice_fusion.mine), channel_id=1, source_target_pairs={{0,8},{8,0},{1,9},{9,1},{2,10},{10,2},{3,11},{11,3},{4,12},{12,4},... | collective-permute-start | bytes 1179656 | tf_op jit(solution)/shard_map/ppermute | solution.py:160
  71.6 6.3 %collective-permute-start.6 = (bf16[16,64,256]{2,1,0:T(8,128)(2,1)S(1)}, bf16[16,64,256]{2,1,0:T(8,128)(2,1)S(1)}, u32[]{:S(2)}, u32[]{:S(2)}) collective-permute-start(bf16[16,64,256]{2,1,0:T(8,128)(2,1)S(1)} %fusion), channel_id=1, source_target_pairs={{0,8},{8,0},{1,9},{9,1},{2,10},{10,2},{3,11},{11,3},{4,12},{12,4},... | collective-permute-start | bytes 1572872 | tf_op jit(solution)/shard_map/ppermute | solution.py:195

commit v4 on v1

v4 whole, which is shorter than its diff:
```python
import functools

import jax
import jax.numpy as jnp
from jax import lax
from jax.experimental import pallas as pl
from jax.experimental.pallas import tpu as pltpu
from jax.sharding import PartitionSpec as P

LOCAL = 4
MAXB = 6
RIM = 8
VMEM_LIMIT = 40 * 1024 * 1024


def vmem():
    return pl.BlockSpec(memory_space=pltpu.VMEM)


def smem():
    return pl.BlockSpec(memory_space=pltpu.SMEM)


def hbm():
    return pl.BlockSpec(memory_space=pltpu.HBM)


def in_hbm(array):
    return pltpu.with_memory_space_constraint(array, pltpu.HBM)


def params():
    return pltpu.CompilerParams(vmem_limit_bytes=VMEM_LIMIT)


def cost(rows, depth, width, moved):
    return pl.CostEstimate(
        flops=2 * rows * depth * width, bytes_accessed=moved, transcendentals=0
    )


def local_kernel(
    orders_in, probes, mixers, gains_in, out, orders, gains, boxes_in, weights, pairs, sems, level_sems
):
    boxes, cols, width = out.shape
    fetches = [
        pltpu.make_async_copy(orders_in, orders, sems.at[0]),
        pltpu.make_async_copy(probes, boxes_in, sems.at[1]),
        pltpu.make_async_copy(gains_in, gains, sems.at[2]),
    ]
    loads = [
        pltpu.make_async_copy(mixers.at[level], weights.at[level], level_sems.at[level])
        for level in range(LOCAL)
    ]
    for copy in fetches + loads:
        copy.start()
    for copy in fetches:
        copy.wait()
    for level in range(LOCAL):
        source = boxes_in if level == 0 else out
        for box in range(boxes):
            block = source[orders[level, box]]
            pairs[box, :, :width] = block
            pairs[box ^ (1 << level), :, width:] = block
        loads[level].wait()
        mixed = jnp.dot(
            pairs[...].reshape(boxes * cols, 2 * width),
            weights[level],
            preferred_element_type=jnp.float32,
        ).reshape(boxes, cols, width)
        out[...] = (mixed * gains[level][:, None, :]).astype(out.dtype)


def cross_kernel(rows, mixers, out, weights, pairs, level_sems):
    count, depth, width = rows.shape
    levels = weights.shape[0]
    loads = [
        pltpu.make_async_copy(mixers.at[LOCAL + level], weights.at[level], level_sems.at[level])
        for level in range(levels)
    ]
    for copy in loads:
        copy.start()
    for level in range(levels):
        source = rows if level == 0 else out
        for box in range(count):
            block = source[box]
            pairs[box, :, :width] = block
            pairs[box ^ (1 << level), :, width:] = block
        loads[level].wait()
        mixed = jnp.dot(
            pairs[...].reshape(count * depth, 2 * width),
            weights[level],
            preferred_element_type=jnp.float32,
        )
        out[...] = mixed.reshape(count, depth, width).astype(out.dtype)


def near_kernel(base, cols_ref, counts, low, own, high, scale, table, out, extended, operand):
    boxes, cols, width = own.shape
    extended[:RIM] = low[...]
    extended[RIM : RIM + boxes] = own[...]
    extended[RIM + boxes :] = high[...]
    first = base[0] - RIM
    for box in range(boxes):
        for slot in range(MAXB):
            block = extended[cols_ref[box, slot] - first].astype(jnp.float32)
            active = (slot < counts[box]).astype(jnp.float32)
            scaled = block * (scale[box, slot : slot + 1, :] * active)
            operand[box, :, slot * width : (slot + 1) * width] = scaled.astype(operand.dtype)
    out[...] = (
        jnp.dot(
            operand[...].reshape(boxes * cols, MAXB * width),
            table[...],
            preferred_element_type=jnp.float32,
        )
        .reshape(boxes, cols, width)
        .astype(out.dtype)
    )


def shards(probes, mixers, box_gains, box_orders, near_count, near_cols, near_scale, near_table):
    boxes, cols, width = probes.shape
    peers = lax.axis_size("bfly")
    levels = mixers.shape[0] - LOCAL
    rows = boxes * cols
    depth = rows // peers
    is_far = lax.axis_index("sec") == 0
    stacked = mixers.reshape(mixers.shape[0], 2 * width, width)

    def far_term(probes):
        current = pl.pallas_call(
            local_kernel,
            out_shape=jax.ShapeDtypeStruct((boxes, cols, width), jnp.bfloat16),
            in_specs=[hbm(), hbm(), hbm(), hbm()],
            out_specs=vmem(),
            scratch_shapes=[
                pltpu.SMEM((LOCAL, boxes), jnp.int32),
                pltpu.VMEM((LOCAL, boxes, width), jnp.float32),
                pltpu.VMEM((boxes, cols, width), jnp.bfloat16),
                pltpu.VMEM((LOCAL, 2 * width, width), jnp.bfloat16),
                pltpu.VMEM((boxes, cols, 2 * width), jnp.bfloat16),
                pltpu.SemaphoreType.DMA((3,)),
                pltpu.SemaphoreType.DMA((LOCAL,)),
            ],
            compiler_params=params(),
            cost_estimate=cost(LOCAL * rows, 2 * width, width, 4 * rows * width),
            name="local_levels",
        )(in_hbm(box_orders), in_hbm(probes), in_hbm(stacked), in_hbm(box_gains))
        spread = lax.all_to_all(current.reshape(peers, depth, width), "bfly", 0, 0, tiled=True)
        crossed = pl.pallas_call(
            cross_kernel,
            out_shape=jax.ShapeDtypeStruct((peers, depth, width), jnp.bfloat16),
            in_specs=[vmem(), hbm()],
            out_specs=vmem(),
            scratch_shapes=[
                pltpu.VMEM((levels, 2 * width, width), jnp.bfloat16),
                pltpu.VMEM((peers, depth, 2 * width), jnp.bfloat16),
                pltpu.SemaphoreType.DMA((levels,)),
            ],
            compiler_params=params(),
            cost_estimate=cost(levels * rows, 2 * width, width, 4 * rows * width),
            name="cross_levels",
        )(spread, in_hbm(stacked))
        back = lax.all_to_all(crossed, "bfly", 0, 0, tiled=True)
        return back.reshape(boxes, cols, width)

    def near_term(probes):
        up = [(i, i + 1) for i in range(peers - 1)]
        down = [(i + 1, i) for i in range(peers - 1)]
        low = lax.ppermute(probes[boxes - RIM :], "bfly", up)
        high = lax.ppermute(probes[:RIM], "bfly", down)
        low, high, piece = lax.optimization_barrier((low, high, near_table))
        table = lax.all_gather(piece, "probe", axis=1, tiled=True)
        return pl.pallas_call(
            near_kernel,
            out_shape=jax.ShapeDtypeStruct((boxes, cols, width), jnp.bfloat16),
            in_specs=[smem(), smem(), smem()] + [vmem()] * 5,
            out_specs=vmem(),
            scratch_shapes=[
                pltpu.VMEM((boxes + 2 * RIM, cols, width), jnp.bfloat16),
                pltpu.VMEM((boxes, cols, MAXB * width), jnp.bfloat16),
            ],
            compiler_params=params(),
            cost_estimate=cost(rows, MAXB * width, width, 8 * rows * width),
            name="near_field",
        )(
            (lax.axis_index("bfly") * boxes)[None],
            near_cols,
            near_count,
            low,
            probes,
            high,
            near_scale,
            table.reshape(MAXB * width, width),
        )

    term = lax.cond(is_far, far_term, near_term, probes)
    other = lax.ppermute(term, "sec", [(0, 1), (1, 0)])
    return term.astype(jnp.float32) + other.astype(jnp.float32)


def solution(mesh):
    return jax.shard_map(
        shards,
        mesh=mesh,
        in_specs=(
            P("bfly", "probe", None),
            P(),
            P(None, "bfly", None),
            P(None, "bfly"),
            P("bfly"),
            P("bfly", None),
            P("bfly", None, None),
            P(None, "probe", None),
        ),
        out_specs=P("bfly", "probe", None),
        check_vma=False,
    )
```

time: 91.2 us -> 74.1 us (0.81)
  the two profiles are of different devices: /device:TPU:31 before, /device:TPU:1 now
where the time goes in v4:
time: 74.1 us; the launch traced here: 73.8 us
  starting transfers between devices  30.1 us (41%)
  blocking collectives  27.4 us (37%)
  waiting for transfers between devices  8.38 us (11%)
  Pallas kernels  3.61 us (5%)
  local copies, waits for them, and re-layouts  2.76 us (4%)
  other arithmetic  1.6 us (2%)
    all_gather x1, blocking collectives, near_term(): table = lax.all_gather(piece, 'probe', axis=1, tiled=True)  27.4 us
    ppermute x1, starting transfers between devices, shards(): other = lax.ppermute(term, 'sec', [(0, 1), (1, 0)])  24.2 us
    ppermute x1, starting transfers between devices, near_term(): low = lax.ppermute(probes[boxes - RIM:], 'bfly', up)  4.61 us
    ppermute x1, waiting for transfers between devices, near_term(): high = lax.ppermute(probes[:RIM], 'bfly', down)  4.43 us
    pallas_call x1, Pallas kernels, near_term(): pl.pallas_call(near_kernel, out_shape=jax.ShapeDtypeStruct((boxes, cols,...  3.61 us
    ppermute x1, waiting for transfers between devices, shards(): other = lax.ppermute(term, 'sec', [(0, 1), (1, 0)])  2.48 us
    add x1, other arithmetic, shards(): return term.astype(jnp.float32) + other.astype(jnp.float32)  1.6 us
  transfers between devices with their start and end apart: 3, of which 3 were waited for; matrix products, arithmetic and copies ran while one was open for 0% of the time, Pallas kernels for 0%

profile of v4, /device:TPU:1, one launch (start us, length us, event | category | flops | bytes accessed | tf_op | source)
XLA Modules:
  0.0 73.8 jit_solution(3310032045600521392)
XLA Ops:
  0.0 45.6 %conditional.4 = (bf16[16,128,256]{2,1,0:T(8,128)(2,1)}, bf16[16,128,256]{2,1,0:T(8,128)(2,1)S(1)}) conditional(s32[]{:T(128)} %convert_element_type.15, (bf16[16,128,256]{2,1,0:T(8,128)(2,1)}, bf16[6,32,256]{2,1,0:T(8,128)(2,1)}, s32[16,6]{0,1:T(8,128)}, s32[16]{0:T(128)}, f32[16,6,256]{2,0,1:T(8,128)}) %tuple.24, (s32[4,16]{1,0:T(4,128)}, ...), branch_computations={%region_0.0_spmd, %region_1.0_spmd} | conditional | flops 4831838208 | bytes 18647832
  0.0 0.0 copy-start.3
  0.0 0.0 copy-start.2
  0.0 0.0 copy-start.1
  0.0 0.0 copy-start
  0.0 0.0 copy-start.4
  0.0 1.4 %fusion = (bf16[8,128,256]{2,1,0:T(8,128)(2,1)S(1)}, bf16[8,128,256]{2,1,0:T(8,128)(2,1)S(1)}) fusion(bf16[16,128,256]{2,1,0:T(8,128)(2,1)} %get-tuple-element.34.own), kind=kLoop, calls=%fused_computation.1 | loop fusion | bytes 2097152 | tf_op jit(solution)/shard_map/cond/branch_0_fun/slice | solution.py:171
  1.4 1.3 %collective-permute-start.1 = (bf16[8,128,256]{2,1,0:T(8,128)(2,1)S(1)}, bf16[8,128,256]{2,1,0:T(8,128)(2,1)S(1)}, u32[]{:S(2)}, u32[]{:S(2)}) collective-permute-start(bf16[8,128,256]{2,1,0:T(8,128)(2,1)S(1)} %get-tuple-element.72), channel_id=1, source_target_pairs={{16,0},{32,16},{48,32},{64,48},{80,64},{96,80},{112,96},{128,112},... | collective-permute-start | bytes 1572872 | tf_op jit(solution)/shard_map/cond/branch_0_fun/ppermute | solution.py:171
  2.7 4.6 %collective-permute-start = (bf16[8,128,256]{2,1,0:T(8,128)(2,1)S(1)}, bf16[8,128,256]{2,1,0:T(8,128)(2,1)S(1)}, u32[]{:S(2)}, u32[]{:S(2)}) collective-permute-start(bf16[8,128,256]{2,1,0:T(8,128)(2,1)S(1)} %get-tuple-element.73), channel_id=1, source_target_pairs={{0,16},{16,32},{32,48},{48,64},{64,80},{80,96},{96,112},{112,128},... | collective-permute-start | bytes 1572872 | tf_op jit(solution)/shard_map/cond/branch_0_fun/ppermute | solution.py:170
  7.3 0.0 copy-done.3
  7.3 0.1 copy.16.cols_ref
  7.4 0.0 copy-done.2
  7.4 0.1 copy.17.scale
  7.5 4.4 %collective-permute-done.1.high = bf16[8,128,256]{2,1,0:T(8,128)(2,1)S(1)} collective-permute-done((bf16[8,128,256]{2,1,0:T(8,128)(2,1)S(1)}, bf16[8,128,256]{2,1,0:T(8,128)(2,1)S(1)}, u32[]{:S(2)}, u32[]{:S(2)}) %collective-permute-start.1) | collective-permute-done | bytes 524320 | tf_op jit(solution)/shard_map/cond/branch_0_fun/ppermute | solution.py:171
  11.9 1.5 %collective-permute-done.low = bf16[8,128,256]{2,1,0:T(8,128)(2,1)S(1)} collective-permute-done((bf16[8,128,256]{2,1,0:T(8,128)(2,1)S(1)}, bf16[8,128,256]{2,1,0:T(8,128)(2,1)S(1)}, u32[]{:S(2)}, u32[]{:S(2)}) %collective-permute-start) | collective-permute-done | bytes 524320 | tf_op jit(solution)/shard_map/cond/branch_0_fun/ppermute | solution.py:170
  13.4 0.0 copy-done.1
  13.4 27.4 %all_gather.2 = bf16[6,256,256]{2,1,0:T(8,128)(2,1)S(1)} all-gather(bf16[6,32,256]{2,1,0:T(8,128)(2,1)S(1)} %copy-done.1), channel_id=1, replica_groups=mesh['bfly'=32,'sec'=2,'probe'=8] {'probe'}, dimensions={1}, use_global_device_ids=true | all-gather | bytes 884736 | tf_op jit(solution)/shard_map/cond/branch_0_fun/all_gather | solution.py:173
  40.8 0.0 copy-done
  40.8 0.0 copy-done.4
  40.8 3.6 %near_field.1 = bf16[16,128,256]{2,1,0:T(8,128)(2,1)} custom-call(s32[1]{0:T(128)} %bitcast.base, s32[16,6]{1,0:T(8,128)S(1)} %copy.16.cols_ref, s32[16]{0:T(128)S(1)} %copy-done.4, bf16[8,128,256]{2,1,0:T(8,128)(2,1)S(1)} %collective-permute-done.low, bf16[16,128,256]{2,1,0:T(8,128)(2,1)S(1)} %copy-done, ...), custom_call_target="tpu_custom_call" | custom-call | flops 1610612736 | bytes 4194304 | tf_op jit(solution)/shard_map/cond/branch_0_fun/near_field/pallas_call | solution.py:174
  44.4 1.2 %copy.19 = bf16[16,128,256]{2,1,0:T(8,128)(2,1)S(1)} copy(bf16[16,128,256]{2,1,0:T(8,128)(2,1)} %near_field.1) | data formatting | bytes 2097152
  45.6 24.2 %collective-permute-start.2 = (bf16[16,128,256]{2,1,0:T(8,128)(2,1)}, bf16[16,128,256]{2,1,0:T(8,128)(2,1)S(1)}, u32[]{:S(2)}, u32[]{:S(2)}) collective-permute-start(bf16[16,128,256]{2,1,0:T(8,128)(2,1)} %get-tuple-element.47), channel_id=1, source_target_pairs={{0,8},{8,0},{1,9},{9,1},{2,10},{10,2},{3,11},{11,3},{4,12},{12,4},... | collective-permute-start | bytes 3145736 | tf_op jit(solution)/shard_map/ppermute | solution.py:198
  69.8 2.5 %collective-permute-done.2 = bf16[16,128,256]{2,1,0:T(8,128)(2,1)S(1)} collective-permute-done((bf16[16,128,256]{2,1,0:T(8,128)(2,1)}, bf16[16,128,256]{2,1,0:T(8,128)(2,1)S(1)}, u32[]{:S(2)}, u32[]{:S(2)}) %collective-permute-start.2) | collective-permute-done | bytes 1048608 | tf_op jit(solution)/shard_map/ppermute | solution.py:198
  72.2 1.6 %convert_add_fusion = f32[16,128,256]{2,1,0:T(8,128)} fusion(bf16[16,128,256]{2,1,0:T(8,128)(2,1)S(1)} %get-tuple-element.71, bf16[16,128,256]{2,1,0:T(8,128)(2,1)S(1)} %collective-permute-done.2), kind=kLoop, calls=%fused_computation | loop fusion | flops 1572864 | bytes 4194304 | tf_op jit(solution)/shard_map/add | solution.py:199
Async XLA Ops:
  0.0 7.3 %copy-start.3 = (s32[16,6]{0,1:T(8,128)S(1)}, s32[16,6]{0,1:T(8,128)}, u32[]{:S(2)}) copy-start(s32[16,6]{0,1:T(8,128)} %get-tuple-element.66) | copy-start | bytes 1156
  0.0 7.4 %copy-start.2 = (f32[16,6,256]{2,0,1:T(8,128)S(1)}, f32[16,6,256]{2,0,1:T(8,128)}, u32[]{:S(2)}) copy-start(f32[16,6,256]{2,0,1:T(8,128)} %get-tuple-element.68) | copy-start | bytes 294916
  0.0 13.4 %copy-start.1 = (bf16[6,32,256]{2,1,0:T(8,128)(2,1)S(1)}, bf16[6,32,256]{2,1,0:T(8,128)(2,1)}, u32[]{:S(2)}) copy-start(bf16[6,32,256]{2,1,0:T(8,128)(2,1)} %get-tuple-element.39) | copy-start | bytes 294916
  0.0 40.8 %copy-start = (bf16[16,128,256]{2,1,0:T(8,128)(2,1)S(1)}, bf16[16,128,256]{2,1,0:T(8,128)(2,1)}, u32[]{:S(2)}) copy-start(bf16[16,128,256]{2,1,0:T(8,128)(2,1)} %get-tuple-element.34.own) | copy-start | bytes 3145732
  0.0 40.7 %copy-start.4 = (s32[16]{0:T(128)S(1)}, s32[16]{0:T(128)}, u32[]{:S(2)}) copy-start(s32[16]{0:T(128)} %get-tuple-element.55.counts) | copy-start | bytes 196
  1.4 10.5 %collective-permute-start.1 = (bf16[8,128,256]{2,1,0:T(8,128)(2,1)S(1)}, bf16[8,128,256]{2,1,0:T(8,128)(2,1)S(1)}, u32[]{:S(2)}, u32[]{:S(2)}) collective-permute-start(bf16[8,128,256]{2,1,0:T(8,128)(2,1)S(1)} %get-tuple-element.72), channel_id=1, source_target_pairs={{16,0},{32,16},{48,32},{64,48},{80,64},{96,80},{112,96},{128,112},... | collective-permute-start | bytes 1572872 | tf_op jit(solution)/shard_map/cond/branch_0_fun/ppermute | solution.py:171
  2.7 10.7 %collective-permute-start = (bf16[8,128,256]{2,1,0:T(8,128)(2,1)S(1)}, bf16[8,128,256]{2,1,0:T(8,128)(2,1)S(1)}, u32[]{:S(2)}, u32[]{:S(2)}) collective-permute-start(bf16[8,128,256]{2,1,0:T(8,128)(2,1)S(1)} %get-tuple-element.73), channel_id=1, source_target_pairs={{0,16},{16,32},{32,48},{48,64},{64,80},{80,96},{96,112},{112,128},... | collective-permute-start | bytes 1572872 | tf_op jit(solution)/shard_map/cond/branch_0_fun/ppermute | solution.py:170
  45.6 26.6 %collective-permute-start.2 = (bf16[16,128,256]{2,1,0:T(8,128)(2,1)}, bf16[16,128,256]{2,1,0:T(8,128)(2,1)S(1)}, u32[]{:S(2)}, u32[]{:S(2)}) collective-permute-start(bf16[16,128,256]{2,1,0:T(8,128)(2,1)} %get-tuple-element.47), channel_id=1, source_target_pairs={{0,8},{8,0},{1,9},{9,1},{2,10},{10,2},{3,11},{11,3},{4,12},{12,4},... | collective-permute-start | bytes 3145736 | tf_op jit(solution)/shard_map/ppermute | solution.py:198

commit v5 on v4

--- a/solution.py
+++ b/solution.py
@@ -10,6 +10,8 @@
 LOCAL = 4
 MAXB = 6
 RIM = 8
+LOCAL_TILE = 2
+CROSS_TILE = 8
 VMEM_LIMIT = 40 * 1024 * 1024
 
 
@@ -63,12 +65,14 @@
             pairs[box, :, :width] = block
             pairs[box ^ (1 << level), :, width:] = block
         loads[level].wait()
-        mixed = jnp.dot(
-            pairs[...].reshape(boxes * cols, 2 * width),
-            weights[level],
-            preferred_element_type=jnp.float32,
-        ).reshape(boxes, cols, width)
-        out[...] = (mixed * gains[level][:, None, :]).astype(out.dtype)
+        for start in range(0, boxes, LOCAL_TILE):
+            tile = slice(start, start + LOCAL_TILE)
+            mixed = jnp.dot(
+                pairs[tile].reshape(LOCAL_TILE * cols, 2 * width),
+                weights[level],
+                preferred_element_type=jnp.float32,
+            ).reshape(LOCAL_TILE, cols, width)
+            out[tile] = (mixed * gains[level, tile][:, None, :]).astype(out.dtype)
 
 
 def cross_kernel(rows, mixers, out, weights, pairs, level_sems):
@@ -87,12 +91,14 @@
             pairs[box, :, :width] = block
             pairs[box ^ (1 << level), :, width:] = block
         loads[level].wait()
-        mixed = jnp.dot(
-            pairs[...].reshape(count * depth, 2 * width),
-            weights[level],
-            preferred_element_type=jnp.float32,
-        )
-        out[...] = mixed.reshape(count, depth, width).astype(out.dtype)
+        for start in range(0, count, CROSS_TILE):
+            tile = slice(start, start + CROSS_TILE)
+            mixed = jnp.dot(
+                pairs[tile].reshape(CROSS_TILE * depth, 2 * width),
+                weights[level],
+                preferred_element_type=jnp.float32,
+            )
+            out[tile] = mixed.reshape(CROSS_TILE, depth, width).astype(out.dtype)
 
 
 def near_kernel(base, cols_ref, counts, low, own, high, scale, table, out, extended, operand):
@@ -124,7 +130,7 @@
     levels = mixers.shape[0] - LOCAL
     rows = boxes * cols
     depth = rows // peers
-    is_far = lax.axis_index("sec") == 0
+    is_far = lax.axis_index("sec") == 1
     stacked = mixers.reshape(mixers.shape[0], 2 * width, width)
 
     def far_term(probes):
@@ -196,6 +202,7 @@
 
     term = lax.cond(is_far, far_term, near_term, probes)
     other = lax.ppermute(term, "sec", [(0, 1), (1, 0)])
+    term = lax.optimization_barrier(term)
     return term.astype(jnp.float32) + other.astype(jnp.float32)
 
 

time: 74.1 us -> 71.9 us (0.970)
  the two profiles are of different devices: /device:TPU:1 before, /device:TPU:33 now
where the time goes in v5:
time: 71.9 us; the launch traced here: 71.7 us
  blocking collectives  49 us (68%)
  starting transfers between devices  9.62 us (13%)
  Pallas kernels  9.15 us (13%)
  waiting for transfers between devices  2.26 us (3%)
  other arithmetic  1.58 us (2%)
    all_to_all x1, blocking collectives, far_term(): back = lax.all_to_all(crossed, 'bfly', 0, 0, tiled=True)  25 us
    all_to_all x1, blocking collectives, far_term(): lax.all_to_all(current.reshape(peers, depth, width), 'bfly', 0, 0, tiled=...  24 us
    ppermute x1, starting transfers between devices, shards(): other = lax.ppermute(term, 'sec', [(0, 1), (1, 0)])  9.62 us
    pallas_call x1, Pallas kernels, far_term(): pl.pallas_call(cross_kernel, out_shape=jax.ShapeDtypeStruct((peers, depth...  4.58 us
    pallas_call x1, Pallas kernels, far_term(): pl.pallas_call(local_kernel, out_shape=jax.ShapeDtypeStruct((boxes, cols,...  4.57 us
    ppermute x1, waiting for transfers between devices, shards(): other = lax.ppermute(term, 'sec', [(0, 1), (1, 0)])  2.26 us
    add x1, other arithmetic, shards(): return term.astype(jnp.float32) + other.astype(jnp.float32)  1.58 us
  transfers between devices with their start and end apart: 1, of which 1 were waited for; matrix products, arithmetic and copies ran while one was open for 0% of the time, Pallas kernels for 0%

profile of v5, /device:TPU:33, one launch (start us, length us, event | category | flops | bytes accessed | tf_op | source)
XLA Modules:
  0.0 71.7 jit_solution(11666732587610017706)
XLA Ops:
  0.0 58.2 %conditional.1 = (bf16[16,128,256]{2,1,0:T(8,128)(2,1)S(1)}) conditional(s32[]{:T(128)} %convert_element_type.9, (bf16[16,128,256]{2,1,0:T(8,128)(2,1)}, bf16[6,32,256]{2,1,0:T(8,128)(2,1)}, s32[16,6]{0,1:T(8,128)}, s32[16]{0:T(128)}, f32[16,6,256]{2,0,1:T(8,128)}) %tuple.12, (s32[4,16]{1,0:T(4,128)}, bf16[16,128,256]{2,1,0:T(8,128)(2,1)}, ...), branch_computations={%region_0.0_spmd, %region_1.0_spmd} | conditional | flops 4831838208 | bytes 16550672 | solution.py:203
  0.0 4.6 %local_levels.1 = bf16[16,128,256]{2,1,0:T(8,128)(2,1)S(1)} custom-call(s32[4,16]{1,0:T(4,128)} %get-tuple-element.49.orders_in, bf16[16,128,256]{2,1,0:T(8,128)(2,1)} %get-tuple-element.35.probes, bf16[9,512,256]{2,1,0:T(8,128)(2,1)} %bitcast.8, f32[4,16,256]{2,1,0:T(8,128)} %get-tuple-element.51.gains_in), custom_call_target="tpu_custom_call" | custom-call | flops 2147483648 | bytes 2097152 | tf_op jit(solution)/shard_map/cond/branch_1_fun/local_levels/pallas_call | solution.py:137
  4.6 24.0 %all_to_all.8.rows = bf16[32,64,256]{2,1,0:T(8,128)(2,1)S(1)} all-to-all(bf16[32,64,256]{2,1,0:T(8,128)(2,1)S(1)} %bitcast.5), channel_id=1, replica_groups=mesh['bfly'=32,'sec'=2,'probe'=8] {'bfly'}, dimensions={0} | all-to-all | bytes 2097152 | tf_op jit(solution)/shard_map/cond/branch_1_fun/all_to_all | solution.py:155
  28.6 4.6 %cross_levels.1 = bf16[32,64,256]{2,1,0:T(8,128)(2,1)S(1)} custom-call(bf16[32,64,256]{2,1,0:T(8,128)(2,1)S(1)} %all_to_all.8.rows, bf16[9,512,256]{2,1,0:T(8,128)(2,1)} %bitcast.9), custom_call_target="tpu_custom_call" | custom-call | flops 2684354560 | bytes 2097152 | tf_op jit(solution)/shard_map/cond/branch_1_fun/cross_levels/pallas_call | solution.py:156
  33.2 25.0 %all_to_all.9 = bf16[32,64,256]{2,1,0:T(8,128)(2,1)S(1)} all-to-all(bf16[32,64,256]{2,1,0:T(8,128)(2,1)S(1)} %cross_levels.1), channel_id=1, replica_groups=mesh['bfly'=32,'sec'=2,'probe'=8] {'bfly'}, dimensions={0} | all-to-all | bytes 2097152 | tf_op jit(solution)/shard_map/cond/branch_1_fun/all_to_all | solution.py:170
  58.2 9.6 %collective-permute-start.2 = (bf16[16,128,256]{2,1,0:T(8,128)(2,1)S(1)}, bf16[16,128,256]{2,1,0:T(8,128)(2,1)S(1)}, u32[]{:S(2)}, u32[]{:S(2)}) collective-permute-start(bf16[16,128,256]{2,1,0:T(8,128)(2,1)S(1)} %get-tuple-element.60), channel_id=1, source_target_pairs={{0,8},{8,0},{1,9},{9,1},{2,10},{10,2},{3,11},{11,3},{4,12},{12,4},... | collective-permute-start | bytes 3145736 | tf_op jit(solution)/shard_map/ppermute | solution.py:204
  67.8 2.3 %collective-permute-done.2 = bf16[16,128,256]{2,1,0:T(8,128)(2,1)S(1)} collective-permute-done((bf16[16,128,256]{2,1,0:T(8,128)(2,1)S(1)}, bf16[16,128,256]{2,1,0:T(8,128)(2,1)S(1)}, u32[]{:S(2)}, u32[]{:S(2)}) %collective-permute-start.2) | collective-permute-done | bytes 1048608 | tf_op jit(solution)/shard_map/ppermute | solution.py:204
  70.1 1.6 %convert_add_fusion = f32[16,128,256]{2,1,0:T(8,128)} fusion(bf16[16,128,256]{2,1,0:T(8,128)(2,1)S(1)} %collective-permute-done.2, bf16[16,128,256]{2,1,0:T(8,128)(2,1)S(1)} %get-tuple-element.60), kind=kLoop, calls=%fused_computation | loop fusion | flops 1572864 | bytes 4194304 | tf_op jit(solution)/shard_map/add | solution.py:206
Async XLA Ops:
  58.2 11.9 %collective-permute-start.2 = (bf16[16,128,256]{2,1,0:T(8,128)(2,1)S(1)}, bf16[16,128,256]{2,1,0:T(8,128)(2,1)S(1)}, u32[]{:S(2)}, u32[]{:S(2)}) collective-permute-start(bf16[16,128,256]{2,1,0:T(8,128)(2,1)S(1)} %get-tuple-element.60), channel_id=1, source_target_pairs={{0,8},{8,0},{1,9},{9,1},{2,10},{10,2},{3,11},{11,3},{4,12},{12,4},... | collective-permute-start | bytes 3145736 | tf_op jit(solution)/shard_map/ppermute | solution.py:204

commit v6 on v5

--- a/solution.py
+++ b/solution.py
@@ -75,27 +75,20 @@
             out[tile] = (mixed * gains[level, tile][:, None, :]).astype(out.dtype)
 
 
-def cross_kernel(rows, mixers, out, weights, pairs, level_sems):
+def cross_kernel(rows, mixers, out, pairs):
     count, depth, width = rows.shape
-    levels = weights.shape[0]
-    loads = [
-        pltpu.make_async_copy(mixers.at[LOCAL + level], weights.at[level], level_sems.at[level])
-        for level in range(levels)
-    ]
-    for copy in loads:
-        copy.start()
+    levels = mixers.shape[0] - LOCAL
     for level in range(levels):
         source = rows if level == 0 else out
         for box in range(count):
             block = source[box]
             pairs[box, :, :width] = block
             pairs[box ^ (1 << level), :, width:] = block
-        loads[level].wait()
         for start in range(0, count, CROSS_TILE):
             tile = slice(start, start + CROSS_TILE)
             mixed = jnp.dot(
                 pairs[tile].reshape(CROSS_TILE * depth, 2 * width),
-                weights[level],
+                mixers[LOCAL + level],
                 preferred_element_type=jnp.float32,
             )
             out[tile] = mixed.reshape(CROSS_TILE, depth, width).astype(out.dtype)
@@ -156,30 +149,26 @@
         crossed = pl.pallas_call(
             cross_kernel,
             out_shape=jax.ShapeDtypeStruct((peers, depth, width), jnp.bfloat16),
-            in_specs=[vmem(), hbm()],
+            in_specs=[vmem(), vmem()],
             out_specs=vmem(),
-            scratch_shapes=[
-                pltpu.VMEM((levels, 2 * width, width), jnp.bfloat16),
-                pltpu.VMEM((peers, depth, 2 * width), jnp.bfloat16),
-                pltpu.SemaphoreType.DMA((levels,)),
-            ],
+            scratch_shapes=[pltpu.VMEM((peers, depth, 2 * width), jnp.bfloat16)],
             compiler_params=params(),
             cost_estimate=cost(levels * rows, 2 * width, width, 4 * rows * width),
             name="cross_levels",
-        )(spread, in_hbm(stacked))
+        )(spread, stacked)
         back = lax.all_to_all(crossed, "bfly", 0, 0, tiled=True)
         return back.reshape(boxes, cols, width)
 
     def near_term(probes):
         up = [(i, i + 1) for i in range(peers - 1)]
         down = [(i + 1, i) for i in range(peers - 1)]
-        low = lax.ppermute(probes[boxes - RIM :], "bfly", up)
-        high = lax.ppermute(probes[:RIM], "bfly", down)
-        low, high, piece = lax.optimization_barrier((low, high, near_table))
-        table = lax.all_gather(piece, "probe", axis=1, tiled=True)
+        table = lax.all_gather(near_table, "probe", axis=1, tiled=True)
+        table, lower, upper = lax.optimization_barrier((table, probes[boxes - RIM :], probes[:RIM]))
+        low = lax.ppermute(lower, "bfly", up)
+        high = lax.ppermute(upper, "bfly", down)
         return pl.pallas_call(
             near_kernel,
-            out_shape=jax.ShapeDtypeStruct((boxes, cols, width), jnp.bfloat16),
+            out_shape=pltpu.VMEM((boxes, cols, width), jnp.bfloat16),
             in_specs=[smem(), smem(), smem()] + [vmem()] * 5,
             out_specs=vmem(),
             scratch_shapes=[

time: 71.9 us -> 69.1 us (0.961)
  the two profiles are of different devices: /device:TPU:33 before, /device:TPU:1 now
where the time goes in v6:
time: 69.1 us; the launch traced here: 67.8 us
  blocking collectives  54 us (78%)
  Pallas kernels  7.61 us (11%)
  waiting for transfers between devices  2.63 us (4%)
  starting transfers between devices  1.91 us (3%)
  other arithmetic  1.6 us (2%)
    all_to_all x1, blocking collectives, far_term(): lax.all_to_all(current.reshape(peers, depth, width), 'bfly', 0, 0, tiled=...  27.5 us
    all_to_all x1, blocking collectives, far_term(): back = lax.all_to_all(crossed, 'bfly', 0, 0, tiled=True)  26.5 us
    pallas_call x1, Pallas kernels, far_term(): pl.pallas_call(local_kernel, out_shape=jax.ShapeDtypeStruct((boxes, cols,...  4.72 us
    pallas_call x1, Pallas kernels, far_term(): pl.pallas_call(cross_kernel, out_shape=jax.ShapeDtypeStruct((peers, depth...  2.89 us
    ppermute x1, waiting for transfers between devices, shards(): other = lax.ppermute(term, 'sec', [(0, 1), (1, 0)])  2.63 us
    ppermute x1, starting transfers between devices, shards(): other = lax.ppermute(term, 'sec', [(0, 1), (1, 0)])  1.91 us
    add x1, other arithmetic, shards(): return term.astype(jnp.float32) + other.astype(jnp.float32)  1.6 us
  transfers between devices with their start and end apart: 1, of which 1 were waited for; matrix products, arithmetic and copies ran while one was open for 0% of the time, Pallas kernels for 0%

profile of v6, /device:TPU:1, one launch (start us, length us, event | category | flops | bytes accessed | tf_op | source)
XLA Modules:
  0.0 67.8 jit_solution(8159685624449076440)
XLA Ops:
  0.0 61.6 %conditional.1 = (bf16[16,128,256]{2,1,0:T(8,128)(2,1)S(1)}) conditional(s32[]{:T(128)} %convert_element_type.9, (bf16[6,32,256]{2,1,0:T(8,128)(2,1)}, bf16[16,128,256]{2,1,0:T(8,128)(2,1)}, s32[16,6]{0,1:T(8,128)}, s32[16]{0:T(128)}, f32[16,6,256]{2,0,1:T(8,128)}) %tuple.12, (s32[4,16]{1,0:T(4,128)}, bf16[16,128,256]{2,1,0:T(8,128)(2,1)}, ...), branch_computations={%region_0.0_spmd, %region_1.0_spmd} | conditional | flops 4831838208 | bytes 17825828 | solution.py:192
  0.0 0.0 copy-start.2
  0.0 4.7 %local_levels.1 = bf16[16,128,256]{2,1,0:T(8,128)(2,1)S(1)} custom-call(s32[4,16]{1,0:T(4,128)} %get-tuple-element.49.orders_in, bf16[16,128,256]{2,1,0:T(8,128)(2,1)} %get-tuple-element.35.probes, bf16[9,512,256]{2,1,0:T(8,128)(2,1)} %bitcast.8, f32[4,16,256]{2,1,0:T(8,128)} %get-tuple-element.51.gains_in), custom_call_target="tpu_custom_call" | custom-call | flops 2147483648 | bytes 2097152 | tf_op jit(solution)/shard_map/cond/branch_1_fun/local_levels/pallas_call | solution.py:130
  4.7 27.5 %all_to_all.8.rows = bf16[32,64,256]{2,1,0:T(8,128)(2,1)S(1)} all-to-all(bf16[32,64,256]{2,1,0:T(8,128)(2,1)S(1)} %bitcast.5), channel_id=1, replica_groups=mesh['bfly'=32,'sec'=2,'probe'=8] {'bfly'}, dimensions={0} | all-to-all | bytes 2097152 | tf_op jit(solution)/shard_map/cond/branch_1_fun/all_to_all | solution.py:148
  32.2 0.0 copy-done.2
  32.2 2.9 %cross_levels.1 = bf16[32,64,256]{2,1,0:T(8,128)(2,1)S(1)} custom-call(bf16[32,64,256]{2,1,0:T(8,128)(2,1)S(1)} %all_to_all.8.rows, bf16[9,512,256]{2,1,0:T(8,128)(2,1)S(1)} %bitcast.9), custom_call_target="tpu_custom_call" | custom-call | flops 2684354560 | bytes 2097152 | tf_op jit(solution)/shard_map/cond/branch_1_fun/cross_levels/pallas_call | solution.py:149
  35.1 26.5 %all_to_all.9 = bf16[32,64,256]{2,1,0:T(8,128)(2,1)S(1)} all-to-all(bf16[32,64,256]{2,1,0:T(8,128)(2,1)S(1)} %cross_levels.1), channel_id=1, replica_groups=mesh['bfly'=32,'sec'=2,'probe'=8] {'bfly'}, dimensions={0} | all-to-all | bytes 2097152 | tf_op jit(solution)/shard_map/cond/branch_1_fun/all_to_all | solution.py:159
  61.6 1.9 %collective-permute-start.2 = (bf16[16,128,256]{2,1,0:T(8,128)(2,1)S(1)}, bf16[16,128,256]{2,1,0:T(8,128)(2,1)S(1)}, u32[]{:S(2)}, u32[]{:S(2)}) collective-permute-start(bf16[16,128,256]{2,1,0:T(8,128)(2,1)S(1)} %get-tuple-element.60), channel_id=1, source_target_pairs={{0,8},{8,0},{1,9},{9,1},{2,10},{10,2},{3,11},{11,3},{4,12},{12,4},... | collective-permute-start | bytes 3145736 | tf_op jit(solution)/shard_map/ppermute | solution.py:193
  63.5 2.6 %collective-permute-done.2 = bf16[16,128,256]{2,1,0:T(8,128)(2,1)S(1)} collective-permute-done((bf16[16,128,256]{2,1,0:T(8,128)(2,1)S(1)}, bf16[16,128,256]{2,1,0:T(8,128)(2,1)S(1)}, u32[]{:S(2)}, u32[]{:S(2)}) %collective-permute-start.2) | collective-permute-done | bytes 1048608 | tf_op jit(solution)/shard_map/ppermute | solution.py:193
  66.2 1.6 %convert_add_fusion = f32[16,128,256]{2,1,0:T(8,128)} fusion(bf16[16,128,256]{2,1,0:T(8,128)(2,1)S(1)} %collective-permute-done.2, bf16[16,128,256]{2,1,0:T(8,128)(2,1)S(1)} %get-tuple-element.60), kind=kLoop, calls=%fused_computation | loop fusion | flops 1572864 | bytes 4194304 | tf_op jit(solution)/shard_map/add | solution.py:195
Async XLA Ops:
  0.0 32.2 %copy-start.2 = (bf16[9,2,256,256]{3,2,1,0:T(8,128)(2,1)S(1)}, bf16[9,2,256,256]{3,2,1,0:T(8,128)(2,1)}, u32[]{:S(2)}) copy-start(bf16[9,2,256,256]{3,2,1,0:T(8,128)(2,1)} %get-tuple-element.52) | copy-start | bytes 7077892 | tf_op jit(solution)/shard_map/cond
  61.6 4.5 %collective-permute-start.2 = (bf16[16,128,256]{2,1,0:T(8,128)(2,1)S(1)}, bf16[16,128,256]{2,1,0:T(8,128)(2,1)S(1)}, u32[]{:S(2)}, u32[]{:S(2)}) collective-permute-start(bf16[16,128,256]{2,1,0:T(8,128)(2,1)S(1)} %get-tuple-element.60), channel_id=1, source_target_pairs={{0,8},{8,0},{1,9},{9,1},{2,10},{10,2},{3,11},{11,3},{4,12},{12,4},... | collective-permute-start | bytes 3145736 | tf_op jit(solution)/shard_map/ppermute | solution.py:193

commit v7 on v6

--- a/solution.py
+++ b/solution.py
@@ -94,8 +94,13 @@
             out[tile] = mixed.reshape(CROSS_TILE, depth, width).astype(out.dtype)
 
 
-def near_kernel(base, cols_ref, counts, low, own, high, scale, table, out, extended, operand):
+def near_kernel(base, cols_ref, counts, low, own, high, scale, parts, out, extended, operand, table):
     boxes, cols, width = own.shape
+    splits, slots, depth, _ = parts.shape
+    for split in range(splits):
+        for slot in range(slots):
+            start = slot * width + split * depth
+            table[start : start + depth] = parts[split, slot]
     extended[:RIM] = low[...]
     extended[RIM : RIM + boxes] = own[...]
     extended[RIM + boxes :] = high[...]
@@ -145,6 +150,7 @@
             cost_estimate=cost(LOCAL * rows, 2 * width, width, 4 * rows * width),
             name="local_levels",
         )(in_hbm(box_orders), in_hbm(probes), in_hbm(stacked), in_hbm(box_gains))
+        current, later = lax.optimization_barrier((current, stacked))
         spread = lax.all_to_all(current.reshape(peers, depth, width), "bfly", 0, 0, tiled=True)
         crossed = pl.pallas_call(
             cross_kernel,
@@ -155,17 +161,18 @@
             compiler_params=params(),
             cost_estimate=cost(levels * rows, 2 * width, width, 4 * rows * width),
             name="cross_levels",
-        )(spread, stacked)
+        )(spread, later)
         back = lax.all_to_all(crossed, "bfly", 0, 0, tiled=True)
         return back.reshape(boxes, cols, width)
 
     def near_term(probes):
         up = [(i, i + 1) for i in range(peers - 1)]
         down = [(i + 1, i) for i in range(peers - 1)]
-        table = lax.all_gather(near_table, "probe", axis=1, tiled=True)
-        table, lower, upper = lax.optimization_barrier((table, probes[boxes - RIM :], probes[:RIM]))
-        low = lax.ppermute(lower, "bfly", up)
-        high = lax.ppermute(upper, "bfly", down)
+        low = lax.ppermute(probes[boxes - RIM :], "bfly", up)
+        high = lax.ppermute(probes[:RIM], "bfly", down)
+        low, high, piece = lax.optimization_barrier((low, high, near_table))
+        copies = jnp.broadcast_to(piece, (lax.axis_size("probe"), *piece.shape))
+        parts = lax.all_to_all(copies, "probe", 0, 0, tiled=True)
         return pl.pallas_call(
             near_kernel,
             out_shape=pltpu.VMEM((boxes, cols, width), jnp.bfloat16),
@@ -174,6 +181,7 @@
             scratch_shapes=[
                 pltpu.VMEM((boxes + 2 * RIM, cols, width), jnp.bfloat16),
                 pltpu.VMEM((boxes, cols, MAXB * width), jnp.bfloat16),
+                pltpu.VMEM((MAXB * width, width), jnp.bfloat16),
             ],
             compiler_params=params(),
             cost_estimate=cost(rows, MAXB * width, width, 8 * rows * width),
@@ -186,7 +194,7 @@
             probes,
             high,
             near_scale,
-            table.reshape(MAXB * width, width),
+            parts,
         )
 
     term = lax.cond(is_far, far_term, near_term, probes)

time: 69.1 us -> 67.7 us (0.980)
  blocking collectives: 54 us -> 52.7 us
    all_to_all x1, blocking collectives: 26.5 us -> 23.8 us  [far_term(): back = lax.all_to_all(crossed, 'bfly', 0, 0, tiled=True)]
    all_to_all x1, blocking collectives: 27.5 us -> 28.9 us  [far_term(): lax.all_to_all(current.reshape(peers, depth, width), 'bfly', 0, 0, tiled=...]
where the time goes in v7:
time: 67.7 us; the launch traced here: 66.5 us
  blocking collectives  52.7 us (78%)
  Pallas kernels  7.61 us (11%)
  waiting for transfers between devices  2.63 us (4%)
  starting transfers between devices  1.91 us (3%)
  other arithmetic  1.6 us (2%)
    all_to_all x1, blocking collectives, far_term(): lax.all_to_all(current.reshape(peers, depth, width), 'bfly', 0, 0, tiled=...  28.9 us
    all_to_all x1, blocking collectives, far_term(): back = lax.all_to_all(crossed, 'bfly', 0, 0, tiled=True)  23.8 us
    pallas_call x1, Pallas kernels, far_term(): pl.pallas_call(local_kernel, out_shape=jax.ShapeDtypeStruct((boxes, cols,...  4.72 us
    pallas_call x1, Pallas kernels, far_term(): pl.pallas_call(cross_kernel, out_shape=jax.ShapeDtypeStruct((peers, depth...  2.89 us
    ppermute x1, waiting for transfers between devices, shards(): other = lax.ppermute(term, 'sec', [(0, 1), (1, 0)])  2.63 us
    ppermute x1, starting transfers between devices, shards(): other = lax.ppermute(term, 'sec', [(0, 1), (1, 0)])  1.91 us
    add x1, other arithmetic, shards(): return term.astype(jnp.float32) + other.astype(jnp.float32)  1.6 us
  transfers between devices with their start and end apart: 1, of which 1 were waited for; matrix products, arithmetic and copies ran while one was open for 0% of the time, Pallas kernels for 0%

profile of v7, /device:TPU:1, one launch (start us, length us, event | category | flops | bytes accessed | tf_op | source)
XLA Modules:
  0.0 66.5 jit_solution(6074416444632574681)
XLA Ops:
  0.0 60.3 %conditional.1 = (bf16[16,128,256]{2,1,0:T(8,128)(2,1)S(1)}) conditional(s32[]{:T(128)} %convert_element_type.9, (bf16[16,128,256]{2,1,0:T(8,128)(2,1)}, bf16[6,32,256]{2,1,0:T(8,128)(2,1)}, s32[16,6]{0,1:T(8,128)}, s32[16]{0:T(128)}, f32[16,6,256]{2,0,1:T(8,128)}) %tuple.13, (s32[4,16]{1,0:T(4,128)}, bf16[16,128,256]{2,1,0:T(8,128)(2,1)}, ...), branch_computations={%region_0.0_spmd, %region_1.0_spmd} | conditional | flops 4831838208 | bytes 17825828 | solution.py:200
  0.0 0.0 copy-start.3
  0.0 4.7 %local_levels.1 = bf16[16,128,256]{2,1,0:T(8,128)(2,1)S(1)} custom-call(s32[4,16]{1,0:T(4,128)} %get-tuple-element.51.orders_in, bf16[16,128,256]{2,1,0:T(8,128)(2,1)} %get-tuple-element.35.probes, bf16[9,512,256]{2,1,0:T(8,128)(2,1)} %bitcast.6, f32[4,16,256]{2,1,0:T(8,128)} %get-tuple-element.53.gains_in), custom_call_target="tpu_custom_call" | custom-call | flops 2147483648 | bytes 2097152 | tf_op jit(solution)/shard_map/cond/branch_1_fun/local_levels/pallas_call | solution.py:135
  4.7 28.9 %all_to_all.12.rows = bf16[32,64,256]{2,1,0:T(8,128)(2,1)S(1)} all-to-all(bf16[32,64,256]{2,1,0:T(8,128)(2,1)S(1)} %bitcast.4), channel_id=1, replica_groups=mesh['bfly'=32,'sec'=2,'probe'=8] {'bfly'}, dimensions={0} | all-to-all | bytes 2097152 | tf_op jit(solution)/shard_map/cond/branch_1_fun/all_to_all | solution.py:154
  33.6 0.0 copy-done.3
  33.6 2.9 %cross_levels.1 = bf16[32,64,256]{2,1,0:T(8,128)(2,1)S(1)} custom-call(bf16[32,64,256]{2,1,0:T(8,128)(2,1)S(1)} %all_to_all.12.rows, bf16[9,512,256]{2,1,0:T(8,128)(2,1)S(1)} %bitcast.7), custom_call_target="tpu_custom_call" | custom-call | flops 2684354560 | bytes 2097152 | tf_op jit(solution)/shard_map/cond/branch_1_fun/cross_levels/pallas_call | solution.py:155
  36.5 23.8 %all_to_all.13 = bf16[32,64,256]{2,1,0:T(8,128)(2,1)S(1)} all-to-all(bf16[32,64,256]{2,1,0:T(8,128)(2,1)S(1)} %cross_levels.1), channel_id=1, replica_groups=mesh['bfly'=32,'sec'=2,'probe'=8] {'bfly'}, dimensions={0} | all-to-all | bytes 2097152 | tf_op jit(solution)/shard_map/cond/branch_1_fun/all_to_all | solution.py:165
  60.3 1.9 %collective-permute-start.2 = (bf16[16,128,256]{2,1,0:T(8,128)(2,1)S(1)}, bf16[16,128,256]{2,1,0:T(8,128)(2,1)S(1)}, u32[]{:S(2)}, u32[]{:S(2)}) collective-permute-start(bf16[16,128,256]{2,1,0:T(8,128)(2,1)S(1)} %get-tuple-element.62), channel_id=1, source_target_pairs={{0,8},{8,0},{1,9},{9,1},{2,10},{10,2},{3,11},{11,3},{4,12},{12,4},... | collective-permute-start | bytes 3145736 | tf_op jit(solution)/shard_map/ppermute | solution.py:201
  62.2 2.6 %collective-permute-done.2 = bf16[16,128,256]{2,1,0:T(8,128)(2,1)S(1)} collective-permute-done((bf16[16,128,256]{2,1,0:T(8,128)(2,1)S(1)}, bf16[16,128,256]{2,1,0:T(8,128)(2,1)S(1)}, u32[]{:S(2)}, u32[]{:S(2)}) %collective-permute-start.2) | collective-permute-done | bytes 1048608 | tf_op jit(solution)/shard_map/ppermute | solution.py:201
  64.9 1.6 %convert_add_fusion = f32[16,128,256]{2,1,0:T(8,128)} fusion(bf16[16,128,256]{2,1,0:T(8,128)(2,1)S(1)} %collective-permute-done.2, bf16[16,128,256]{2,1,0:T(8,128)(2,1)S(1)} %get-tuple-element.62), kind=kLoop, calls=%fused_computation | loop fusion | flops 1572864 | bytes 4194304 | tf_op jit(solution)/shard_map/add | solution.py:203
Async XLA Ops:
  0.0 33.6 %copy-start.3 = (bf16[9,2,256,256]{3,2,1,0:T(8,128)(2,1)S(1)}, bf16[9,2,256,256]{3,2,1,0:T(8,128)(2,1)}, u32[]{:S(2)}) copy-start(bf16[9,2,256,256]{3,2,1,0:T(8,128)(2,1)} %get-tuple-element.54) | copy-start | bytes 7077892 | tf_op jit(solution)/shard_map/cond
  60.3 4.5 %collective-permute-start.2 = (bf16[16,128,256]{2,1,0:T(8,128)(2,1)S(1)}, bf16[16,128,256]{2,1,0:T(8,128)(2,1)S(1)}, u32[]{:S(2)}, u32[]{:S(2)}) collective-permute-start(bf16[16,128,256]{2,1,0:T(8,128)(2,1)S(1)} %get-tuple-element.62), channel_id=1, source_target_pairs={{0,8},{8,0},{1,9},{9,1},{2,10},{10,2},{3,11},{11,3},{4,12},{12,4},... | collective-permute-start | bytes 3145736 | tf_op jit(solution)/shard_map/ppermute | solution.py:201

commit v8 on v7

--- a/solution.py
+++ b/solution.py
@@ -170,8 +170,7 @@
         down = [(i + 1, i) for i in range(peers - 1)]
         low = lax.ppermute(probes[boxes - RIM :], "bfly", up)
         high = lax.ppermute(probes[:RIM], "bfly", down)
-        low, high, piece = lax.optimization_barrier((low, high, near_table))
-        copies = jnp.broadcast_to(piece, (lax.axis_size("probe"), *piece.shape))
+        copies = jnp.broadcast_to(near_table, (lax.axis_size("probe"), *near_table.shape))
         parts = lax.all_to_all(copies, "probe", 0, 0, tiled=True)
         return pl.pallas_call(
             near_kernel,

time: 67.7 us -> 67.3 us (level)
  the two profiles are of different devices: /device:TPU:1 before, /device:TPU:451 now
where the time goes in v8:
time: 67.3 us; the launch traced here: 67 us
  blocking collectives  53.3 us (79%)
  Pallas kernels  7.6 us (11%)
  waiting for transfers between devices  2.63 us (4%)
  starting transfers between devices  1.91 us (3%)
  other arithmetic  1.6 us (2%)
    all_to_all x1, blocking collectives, far_term(): lax.all_to_all(current.reshape(peers, depth, width), 'bfly', 0, 0, tiled=...  27.7 us
    all_to_all x1, blocking collectives, far_term(): back = lax.all_to_all(crossed, 'bfly', 0, 0, tiled=True)  25.5 us
    pallas_call x1, Pallas kernels, far_term(): pl.pallas_call(local_kernel, out_shape=jax.ShapeDtypeStruct((boxes, cols,...  4.72 us
    pallas_call x1, Pallas kernels, far_term(): pl.pallas_call(cross_kernel, out_shape=jax.ShapeDtypeStruct((peers, depth...  2.89 us
    ppermute x1, waiting for transfers between devices, shards(): other = lax.ppermute(term, 'sec', [(0, 1), (1, 0)])  2.63 us
    ppermute x1, starting transfers between devices, shards(): other = lax.ppermute(term, 'sec', [(0, 1), (1, 0)])  1.91 us
    add x1, other arithmetic, shards(): return term.astype(jnp.float32) + other.astype(jnp.float32)  1.6 us
  transfers between devices with their start and end apart: 1, of which 1 were waited for; matrix products, arithmetic and copies ran while one was open for 0% of the time, Pallas kernels for 0%

profile of v8, /device:TPU:451, one launch (start us, length us, event | category | flops | bytes accessed | tf_op | source)
XLA Modules:
  0.0 67.0 jit_solution(8651832516905250728)
XLA Ops:
  0.0 60.9 %conditional.1 = (bf16[16,128,256]{2,1,0:T(8,128)(2,1)S(1)}) conditional(s32[]{:T(128)} %convert_element_type.9, (bf16[16,128,256]{2,1,0:T(8,128)(2,1)}, bf16[6,32,256]{2,1,0:T(8,128)(2,1)}, s32[16,6]{0,1:T(8,128)}, s32[16]{0:T(128)}, f32[16,6,256]{2,0,1:T(8,128)}) %tuple.12, (s32[4,16]{1,0:T(4,128)}, bf16[16,128,256]{2,1,0:T(8,128)(2,1)}, ...), branch_computations={%region_0.0_spmd, %region_1.0_spmd} | conditional | flops 4831838208 | bytes 18516756 | solution.py:199
  0.0 0.0 copy-start.3
  0.0 4.7 %local_levels.1 = bf16[16,128,256]{2,1,0:T(8,128)(2,1)S(1)} custom-call(s32[4,16]{1,0:T(4,128)} %get-tuple-element.48.orders_in, bf16[16,128,256]{2,1,0:T(8,128)(2,1)} %get-tuple-element.32.probes, bf16[9,512,256]{2,1,0:T(8,128)(2,1)} %bitcast.6, f32[4,16,256]{2,1,0:T(8,128)} %get-tuple-element.50.gains_in), custom_call_target="tpu_custom_call" | custom-call | flops 2147483648 | bytes 2097152 | tf_op jit(solution)/shard_map/cond/branch_1_fun/local_levels/pallas_call | solution.py:135
  4.7 27.7 %all_to_all.12.rows = bf16[32,64,256]{2,1,0:T(8,128)(2,1)S(1)} all-to-all(bf16[32,64,256]{2,1,0:T(8,128)(2,1)S(1)} %bitcast.4), channel_id=1, replica_groups=mesh['bfly'=32,'sec'=2,'probe'=8] {'bfly'}, dimensions={0} | all-to-all | bytes 2097152 | tf_op jit(solution)/shard_map/cond/branch_1_fun/all_to_all | solution.py:154
  32.5 0.0 copy-done.3
  32.5 2.9 %cross_levels.1 = bf16[32,64,256]{2,1,0:T(8,128)(2,1)S(1)} custom-call(bf16[32,64,256]{2,1,0:T(8,128)(2,1)S(1)} %all_to_all.12.rows, bf16[9,512,256]{2,1,0:T(8,128)(2,1)S(1)} %bitcast.7), custom_call_target="tpu_custom_call" | custom-call | flops 2684354560 | bytes 2097152 | tf_op jit(solution)/shard_map/cond/branch_1_fun/cross_levels/pallas_call | solution.py:155
  35.4 25.5 %all_to_all.13 = bf16[32,64,256]{2,1,0:T(8,128)(2,1)S(1)} all-to-all(bf16[32,64,256]{2,1,0:T(8,128)(2,1)S(1)} %cross_levels.1), channel_id=1, replica_groups=mesh['bfly'=32,'sec'=2,'probe'=8] {'bfly'}, dimensions={0} | all-to-all | bytes 2097152 | tf_op jit(solution)/shard_map/cond/branch_1_fun/all_to_all | solution.py:165
  60.9 1.9 %collective-permute-start.2 = (bf16[16,128,256]{2,1,0:T(8,128)(2,1)S(1)}, bf16[16,128,256]{2,1,0:T(8,128)(2,1)S(1)}, u32[]{:S(2)}, u32[]{:S(2)}) collective-permute-start(bf16[16,128,256]{2,1,0:T(8,128)(2,1)S(1)} %get-tuple-element.59), channel_id=1, source_target_pairs={{0,8},{8,0},{1,9},{9,1},{2,10},{10,2},{3,11},{11,3},{4,12},{12,4},... | collective-permute-start | bytes 3145736 | tf_op jit(solution)/shard_map/ppermute | solution.py:200
  62.8 2.6 %collective-permute-done.2 = bf16[16,128,256]{2,1,0:T(8,128)(2,1)S(1)} collective-permute-done((bf16[16,128,256]{2,1,0:T(8,128)(2,1)S(1)}, bf16[16,128,256]{2,1,0:T(8,128)(2,1)S(1)}, u32[]{:S(2)}, u32[]{:S(2)}) %collective-permute-start.2) | collective-permute-done | bytes 1048608 | tf_op jit(solution)/shard_map/ppermute | solution.py:200
  65.4 1.6 %convert_add_fusion = f32[16,128,256]{2,1,0:T(8,128)} fusion(bf16[16,128,256]{2,1,0:T(8,128)(2,1)S(1)} %collective-permute-done.2, bf16[16,128,256]{2,1,0:T(8,128)(2,1)S(1)} %get-tuple-element.59), kind=kLoop, calls=%fused_computation | loop fusion | flops 1572864 | bytes 4194304 | tf_op jit(solution)/shard_map/add | solution.py:202
Async XLA Ops:
  0.0 32.5 %copy-start.3 = (bf16[9,2,256,256]{3,2,1,0:T(8,128)(2,1)S(1)}, bf16[9,2,256,256]{3,2,1,0:T(8,128)(2,1)}, u32[]{:S(2)}) copy-start(bf16[9,2,256,256]{3,2,1,0:T(8,128)(2,1)} %get-tuple-element.51) | copy-start | bytes 7077892 | tf_op jit(solution)/shard_map/cond
  60.9 4.5 %collective-permute-start.2 = (bf16[16,128,256]{2,1,0:T(8,128)(2,1)S(1)}, bf16[16,128,256]{2,1,0:T(8,128)(2,1)S(1)}, u32[]{:S(2)}, u32[]{:S(2)}) collective-permute-start(bf16[16,128,256]{2,1,0:T(8,128)(2,1)S(1)} %get-tuple-element.59), channel_id=1, source_target_pairs={{0,8},{8,0},{1,9},{9,1},{2,10},{10,2},{3,11},{11,3},{4,12},{12,4},... | collective-permute-start | bytes 3145736 | tf_op jit(solution)/shard_map/ppermute | solution.py:200

commit v9 on v8

--- a/solution.py
+++ b/solution.py
@@ -168,10 +168,13 @@
     def near_term(probes):
         up = [(i, i + 1) for i in range(peers - 1)]
         down = [(i + 1, i) for i in range(peers - 1)]
-        low = lax.ppermute(probes[boxes - RIM :], "bfly", up)
-        high = lax.ppermute(probes[:RIM], "bfly", down)
         copies = jnp.broadcast_to(near_table, (lax.axis_size("probe"), *near_table.shape))
         parts = lax.all_to_all(copies, "probe", 0, 0, tiled=True)
+        parts, lower, upper = lax.optimization_barrier(
+            (parts, probes[boxes - RIM :], probes[:RIM])
+        )
+        low = lax.ppermute(lower, "bfly", up)
+        high = lax.ppermute(upper, "bfly", down)
         return pl.pallas_call(
             near_kernel,
             out_shape=pltpu.VMEM((boxes, cols, width), jnp.bfloat16),

time: 67.3 us -> 68.7 us (1.021)
  the two profiles are of different devices: /device:TPU:451 before, /device:TPU:31 now
where the time goes in v9:
time: 68.7 us; the launch traced here: 68.5 us
  blocking collectives  47.2 us (69%)
  starting transfers between devices  9.76 us (14%)
  Pallas kernels  7.6 us (11%)
  waiting for transfers between devices  2.26 us (3%)
  other arithmetic  1.6 us (2%)
    all_to_all x1, blocking collectives, far_term(): lax.all_to_all(current.reshape(peers, depth, width), 'bfly', 0, 0, tiled=...  24.1 us
    all_to_all x1, blocking collectives, far_term(): back = lax.all_to_all(crossed, 'bfly', 0, 0, tiled=True)  23.1 us
    ppermute x1, starting transfers between devices, shards(): other = lax.ppermute(term, 'sec', [(0, 1), (1, 0)])  9.76 us
    pallas_call x1, Pallas kernels, far_term(): pl.pallas_call(local_kernel, out_shape=jax.ShapeDtypeStruct((boxes, cols,...  4.72 us
    pallas_call x1, Pallas kernels, far_term(): pl.pallas_call(cross_kernel, out_shape=jax.ShapeDtypeStruct((peers, depth...  2.89 us
    ppermute x1, waiting for transfers between devices, shards(): other = lax.ppermute(term, 'sec', [(0, 1), (1, 0)])  2.26 us
    add x1, other arithmetic, shards(): return term.astype(jnp.float32) + other.astype(jnp.float32)  1.6 us
  transfers between devices with their start and end apart: 1, of which 1 were waited for; matrix products, arithmetic and copies ran while one was open for 0% of the time, Pallas kernels for 0%

profile of v9, /device:TPU:31, one launch (start us, length us, event | category | flops | bytes accessed | tf_op | source)
XLA Modules:
  0.0 68.5 jit_solution(18318127708492281356)
XLA Ops:
  0.0 54.8 %conditional.1 = (bf16[16,128,256]{2,1,0:T(8,128)(2,1)S(1)}) conditional(s32[]{:T(128)} %convert_element_type.9, (bf16[6,32,256]{2,1,0:T(8,128)(2,1)}, bf16[16,128,256]{2,1,0:T(8,128)(2,1)}, s32[16,6]{0,1:T(8,128)}, s32[16]{0:T(128)}, f32[16,6,256]{2,0,1:T(8,128)}) %tuple.13, (s32[4,16]{1,0:T(4,128)}, bf16[16,128,256]{2,1,0:T(8,128)(2,1)}, ...), branch_computations={%region_0.0_spmd, %region_1.0_spmd} | conditional | flops 4831838208 | bytes 18516756 | solution.py:202
  0.0 0.0 copy-start.3
  0.0 4.7 %local_levels.1 = bf16[16,128,256]{2,1,0:T(8,128)(2,1)S(1)} custom-call(s32[4,16]{1,0:T(4,128)} %get-tuple-element.51.orders_in, bf16[16,128,256]{2,1,0:T(8,128)(2,1)} %get-tuple-element.35.probes, bf16[9,512,256]{2,1,0:T(8,128)(2,1)} %bitcast.6, f32[4,16,256]{2,1,0:T(8,128)} %get-tuple-element.53.gains_in), custom_call_target="tpu_custom_call" | custom-call | flops 2147483648 | bytes 2097152 | tf_op jit(solution)/shard_map/cond/branch_1_fun/local_levels/pallas_call | solution.py:135
  4.7 24.1 %all_to_all.12.rows = bf16[32,64,256]{2,1,0:T(8,128)(2,1)S(1)} all-to-all(bf16[32,64,256]{2,1,0:T(8,128)(2,1)S(1)} %bitcast.4), channel_id=1, replica_groups=mesh['bfly'=32,'sec'=2,'probe'=8] {'bfly'}, dimensions={0} | all-to-all | bytes 2097152 | tf_op jit(solution)/shard_map/cond/branch_1_fun/all_to_all | solution.py:154
  28.8 0.0 copy-done.3
  28.8 2.9 %cross_levels.1 = bf16[32,64,256]{2,1,0:T(8,128)(2,1)S(1)} custom-call(bf16[32,64,256]{2,1,0:T(8,128)(2,1)S(1)} %all_to_all.12.rows, bf16[9,512,256]{2,1,0:T(8,128)(2,1)S(1)} %bitcast.7), custom_call_target="tpu_custom_call" | custom-call | flops 2684354560 | bytes 2097152 | tf_op jit(solution)/shard_map/cond/branch_1_fun/cross_levels/pallas_call | solution.py:155
  31.7 23.1 %all_to_all.13 = bf16[32,64,256]{2,1,0:T(8,128)(2,1)S(1)} all-to-all(bf16[32,64,256]{2,1,0:T(8,128)(2,1)S(1)} %cross_levels.1), channel_id=1, replica_groups=mesh['bfly'=32,'sec'=2,'probe'=8] {'bfly'}, dimensions={0} | all-to-all | bytes 2097152 | tf_op jit(solution)/shard_map/cond/branch_1_fun/all_to_all | solution.py:165
  54.8 9.8 %collective-permute-start.2 = (bf16[16,128,256]{2,1,0:T(8,128)(2,1)S(1)}, bf16[16,128,256]{2,1,0:T(8,128)(2,1)S(1)}, u32[]{:S(2)}, u32[]{:S(2)}) collective-permute-start(bf16[16,128,256]{2,1,0:T(8,128)(2,1)S(1)} %get-tuple-element.62), channel_id=1, source_target_pairs={{0,8},{8,0},{1,9},{9,1},{2,10},{10,2},{3,11},{11,3},{4,12},{12,4},... | collective-permute-start | bytes 3145736 | tf_op jit(solution)/shard_map/ppermute | solution.py:203
  64.6 2.3 %collective-permute-done.2 = bf16[16,128,256]{2,1,0:T(8,128)(2,1)S(1)} collective-permute-done((bf16[16,128,256]{2,1,0:T(8,128)(2,1)S(1)}, bf16[16,128,256]{2,1,0:T(8,128)(2,1)S(1)}, u32[]{:S(2)}, u32[]{:S(2)}) %collective-permute-start.2) | collective-permute-done | bytes 1048608 | tf_op jit(solution)/shard_map/ppermute | solution.py:203
  66.9 1.6 %convert_add_fusion = f32[16,128,256]{2,1,0:T(8,128)} fusion(bf16[16,128,256]{2,1,0:T(8,128)(2,1)S(1)} %collective-permute-done.2, bf16[16,128,256]{2,1,0:T(8,128)(2,1)S(1)} %get-tuple-element.62), kind=kLoop, calls=%fused_computation | loop fusion | flops 1572864 | bytes 4194304 | tf_op jit(solution)/shard_map/add | solution.py:205
Async XLA Ops:
  0.0 28.8 %copy-start.3 = (bf16[9,2,256,256]{3,2,1,0:T(8,128)(2,1)S(1)}, bf16[9,2,256,256]{3,2,1,0:T(8,128)(2,1)}, u32[]{:S(2)}) copy-start(bf16[9,2,256,256]{3,2,1,0:T(8,128)(2,1)} %get-tuple-element.54) | copy-start | bytes 7077892 | tf_op jit(solution)/shard_map/cond
  54.8 12.0 %collective-permute-start.2 = (bf16[16,128,256]{2,1,0:T(8,128)(2,1)S(1)}, bf16[16,128,256]{2,1,0:T(8,128)(2,1)S(1)}, u32[]{:S(2)}, u32[]{:S(2)}) collective-permute-start(bf16[16,128,256]{2,1,0:T(8,128)(2,1)S(1)} %get-tuple-element.62), channel_id=1, source_target_pairs={{0,8},{8,0},{1,9},{9,1},{2,10},{10,2},{3,11},{11,3},{4,12},{12,4},... | collective-permute-start | bytes 3145736 | tf_op jit(solution)/shard_map/ppermute | solution.py:203

commit v10 on v8

--- a/solution.py
+++ b/solution.py
@@ -168,10 +168,11 @@
     def near_term(probes):
         up = [(i, i + 1) for i in range(peers - 1)]
         down = [(i + 1, i) for i in range(peers - 1)]
-        low = lax.ppermute(probes[boxes - RIM :], "bfly", up)
-        high = lax.ppermute(probes[:RIM], "bfly", down)
         copies = jnp.broadcast_to(near_table, (lax.axis_size("probe"), *near_table.shape))
         parts = lax.all_to_all(copies, "probe", 0, 0, tiled=True)
+        parts, upper = lax.optimization_barrier((parts, probes[:RIM]))
+        low = lax.ppermute(probes[boxes - RIM :], "bfly", up)
+        high = lax.ppermute(upper, "bfly", down)
         return pl.pallas_call(
             near_kernel,
             out_shape=pltpu.VMEM((boxes, cols, width), jnp.bfloat16),

time: 67.3 us -> 67.8 us (level)
  the two profiles are of different devices: /device:TPU:451 before, /device:TPU:1 now
where the time goes in v10:
time: 67.8 us; the launch traced here: 66.8 us
  blocking collectives  53.1 us (78%)
  Pallas kernels  7.6 us (11%)
  waiting for transfers between devices  2.63 us (4%)
  starting transfers between devices  1.91 us (3%)
  other arithmetic  1.6 us (2%)
    all_to_all x1, blocking collectives, far_term(): lax.all_to_all(current.reshape(peers, depth, width), 'bfly', 0, 0, tiled=...  31 us
    all_to_all x1, blocking collectives, far_term(): back = lax.all_to_all(crossed, 'bfly', 0, 0, tiled=True)  22.1 us
    pallas_call x1, Pallas kernels, far_term(): pl.pallas_call(local_kernel, out_shape=jax.ShapeDtypeStruct((boxes, cols,...  4.72 us
    pallas_call x1, Pallas kernels, far_term(): pl.pallas_call(cross_kernel, out_shape=jax.ShapeDtypeStruct((peers, depth...  2.89 us
    ppermute x1, waiting for transfers between devices, shards(): other = lax.ppermute(term, 'sec', [(0, 1), (1, 0)])  2.63 us
    ppermute x1, starting transfers between devices, shards(): other = lax.ppermute(term, 'sec', [(0, 1), (1, 0)])  1.91 us
    add x1, other arithmetic, shards(): return term.astype(jnp.float32) + other.astype(jnp.float32)  1.6 us
  transfers between devices with their start and end apart: 1, of which 1 were waited for; matrix products, arithmetic and copies ran while one was open for 0% of the time, Pallas kernels for 0%

profile of v10, /device:TPU:1, one launch (start us, length us, event | category | flops | bytes accessed | tf_op | source)
XLA Modules:
  0.0 66.8 jit_solution(6018847927599583317)
XLA Ops:
  0.0 60.7 %conditional.1 = (bf16[16,128,256]{2,1,0:T(8,128)(2,1)S(1)}) conditional(s32[]{:T(128)} %convert_element_type.9, (bf16[16,128,256]{2,1,0:T(8,128)(2,1)}, bf16[6,32,256]{2,1,0:T(8,128)(2,1)}, s32[16,6]{0,1:T(8,128)}, s32[16]{0:T(128)}, f32[16,6,256]{2,0,1:T(8,128)}) %tuple.13, (s32[4,16]{1,0:T(4,128)}, bf16[16,128,256]{2,1,0:T(8,128)(2,1)}, ...), branch_computations={%region_0.0_spmd, %region_1.0_spmd} | conditional | flops 4831838208 | bytes 18516756 | solution.py:200
  0.0 0.0 copy-start.3
  0.0 4.7 %local_levels.1 = bf16[16,128,256]{2,1,0:T(8,128)(2,1)S(1)} custom-call(s32[4,16]{1,0:T(4,128)} %get-tuple-element.50.orders_in, bf16[16,128,256]{2,1,0:T(8,128)(2,1)} %get-tuple-element.34.probes, bf16[9,512,256]{2,1,0:T(8,128)(2,1)} %bitcast.6, f32[4,16,256]{2,1,0:T(8,128)} %get-tuple-element.52.gains_in), custom_call_target="tpu_custom_call" | custom-call | flops 2147483648 | bytes 2097152 | tf_op jit(solution)/shard_map/cond/branch_1_fun/local_levels/pallas_call | solution.py:135
  4.7 31.0 %all_to_all.12.rows = bf16[32,64,256]{2,1,0:T(8,128)(2,1)S(1)} all-to-all(bf16[32,64,256]{2,1,0:T(8,128)(2,1)S(1)} %bitcast.4), channel_id=1, replica_groups=mesh['bfly'=32,'sec'=2,'probe'=8] {'bfly'}, dimensions={0} | all-to-all | bytes 2097152 | tf_op jit(solution)/shard_map/cond/branch_1_fun/all_to_all | solution.py:154
  35.7 0.0 copy-done.3
  35.7 2.9 %cross_levels.1 = bf16[32,64,256]{2,1,0:T(8,128)(2,1)S(1)} custom-call(bf16[32,64,256]{2,1,0:T(8,128)(2,1)S(1)} %all_to_all.12.rows, bf16[9,512,256]{2,1,0:T(8,128)(2,1)S(1)} %bitcast.7), custom_call_target="tpu_custom_call" | custom-call | flops 2684354560 | bytes 2097152 | tf_op jit(solution)/shard_map/cond/branch_1_fun/cross_levels/pallas_call | solution.py:155
  38.6 22.1 %all_to_all.13 = bf16[32,64,256]{2,1,0:T(8,128)(2,1)S(1)} all-to-all(bf16[32,64,256]{2,1,0:T(8,128)(2,1)S(1)} %cross_levels.1), channel_id=1, replica_groups=mesh['bfly'=32,'sec'=2,'probe'=8] {'bfly'}, dimensions={0} | all-to-all | bytes 2097152 | tf_op jit(solution)/shard_map/cond/branch_1_fun/all_to_all | solution.py:165
  60.7 1.9 %collective-permute-start.2 = (bf16[16,128,256]{2,1,0:T(8,128)(2,1)S(1)}, bf16[16,128,256]{2,1,0:T(8,128)(2,1)S(1)}, u32[]{:S(2)}, u32[]{:S(2)}) collective-permute-start(bf16[16,128,256]{2,1,0:T(8,128)(2,1)S(1)} %get-tuple-element.61), channel_id=1, source_target_pairs={{0,8},{8,0},{1,9},{9,1},{2,10},{10,2},{3,11},{11,3},{4,12},{12,4},... | collective-permute-start | bytes 3145736 | tf_op jit(solution)/shard_map/ppermute | solution.py:201
  62.6 2.6 %collective-permute-done.2 = bf16[16,128,256]{2,1,0:T(8,128)(2,1)S(1)} collective-permute-done((bf16[16,128,256]{2,1,0:T(8,128)(2,1)S(1)}, bf16[16,128,256]{2,1,0:T(8,128)(2,1)S(1)}, u32[]{:S(2)}, u32[]{:S(2)}) %collective-permute-start.2) | collective-permute-done | bytes 1048608 | tf_op jit(solution)/shard_map/ppermute | solution.py:201
  65.2 1.6 %convert_add_fusion = f32[16,128,256]{2,1,0:T(8,128)} fusion(bf16[16,128,256]{2,1,0:T(8,128)(2,1)S(1)} %collective-permute-done.2, bf16[16,128,256]{2,1,0:T(8,128)(2,1)S(1)} %get-tuple-element.61), kind=kLoop, calls=%fused_computation | loop fusion | flops 1572864 | bytes 4194304 | tf_op jit(solution)/shard_map/add | solution.py:203
Async XLA Ops:
  0.0 35.7 %copy-start.3 = (bf16[9,2,256,256]{3,2,1,0:T(8,128)(2,1)S(1)}, bf16[9,2,256,256]{3,2,1,0:T(8,128)(2,1)}, u32[]{:S(2)}) copy-start(bf16[9,2,256,256]{3,2,1,0:T(8,128)(2,1)} %get-tuple-element.53) | copy-start | bytes 7077892 | tf_op jit(solution)/shard_map/cond
  60.7 4.5 %collective-permute-start.2 = (bf16[16,128,256]{2,1,0:T(8,128)(2,1)S(1)}, bf16[16,128,256]{2,1,0:T(8,128)(2,1)S(1)}, u32[]{:S(2)}, u32[]{:S(2)}) collective-permute-start(bf16[16,128,256]{2,1,0:T(8,128)(2,1)S(1)} %get-tuple-element.61), channel_id=1, source_target_pairs={{0,8},{8,0},{1,9},{9,1},{2,10},{10,2},{3,11},{11,3},{4,12},{12,4},... | collective-permute-start | bytes 3145736 | tf_op jit(solution)/shard_map/ppermute | solution.py:201

commit v11 on v8

--- a/solution.py
+++ b/solution.py
@@ -12,6 +12,7 @@
 RIM = 8
 LOCAL_TILE = 2
 CROSS_TILE = 8
+SUM_TILE = 2
 VMEM_LIMIT = 40 * 1024 * 1024
 
 
@@ -120,6 +121,18 @@
         .reshape(boxes, cols, width)
         .astype(out.dtype)
     )
+
+
+def sum_kernel(mine, other, out, total, sems):
+    stores = []
+    for start in range(0, out.shape[0], SUM_TILE):
+        tile = pl.ds(start, SUM_TILE)
+        total[tile] = mine[tile].astype(jnp.float32) + other[tile].astype(jnp.float32)
+        store = pltpu.make_async_copy(total.at[tile], out.at[tile], sems.at[start // SUM_TILE])
+        store.start()
+        stores.append(store)
+    for store in stores:
+        store.wait()
 
 
 def shards(probes, mixers, box_gains, box_orders, near_count, near_cols, near_scale, near_table):
@@ -199,7 +212,19 @@
     term = lax.cond(is_far, far_term, near_term, probes)
     other = lax.ppermute(term, "sec", [(0, 1), (1, 0)])
     term = lax.optimization_barrier(term)
-    return term.astype(jnp.float32) + other.astype(jnp.float32)
+    return pl.pallas_call(
+        sum_kernel,
+        out_shape=pltpu.HBM((boxes, cols, width), jnp.float32),
+        in_specs=[vmem(), vmem()],
+        out_specs=hbm(),
+        scratch_shapes=[
+            pltpu.VMEM((boxes, cols, width), jnp.float32),
+            pltpu.SemaphoreType.DMA((boxes // SUM_TILE,)),
+        ],
+        compiler_params=params(),
+        cost_estimate=cost(rows, 1, width, 8 * rows * width),
+        name="response_sum",
+    )(term, other)
 
 
 def solution(mesh):

time: 67.3 us -> 67.2 us (level)
  other arithmetic: 1.6 us -> 0 us
  Pallas kernels: 7.6 us -> 9.01 us
    add x1 -> x0, other arithmetic: 1.6 us -> none  [shards(): return term.astype(jnp.float32) + other.astype(jnp.float32)]
    pallas_call x0 -> x1, Pallas kernels: none -> 1.4 us  [shards(): pl.pallas_call(sum_kernel, out_shape=pltpu.HBM((boxes, cols, width), jnp....]
where the time goes in v11:
time: 67.2 us; the launch traced here: 66.9 us
  blocking collectives  53.3 us (79%)
  Pallas kernels  9.01 us (13%)
  waiting for transfers between devices  2.63 us (4%)
  starting transfers between devices  1.91 us (3%)
    all_to_all x1, blocking collectives, far_term(): lax.all_to_all(current.reshape(peers, depth, width), 'bfly', 0, 0, tiled=...  27.5 us
    all_to_all x1, blocking collectives, far_term(): back = lax.all_to_all(crossed, 'bfly', 0, 0, tiled=True)  25.8 us
    pallas_call x1, Pallas kernels, far_term(): pl.pallas_call(local_kernel, out_shape=jax.ShapeDtypeStruct((boxes, cols,...  4.72 us
    pallas_call x1, Pallas kernels, far_term(): pl.pallas_call(cross_kernel, out_shape=jax.ShapeDtypeStruct((peers, depth...  2.89 us
    ppermute x1, waiting for transfers between devices, shards(): other = lax.ppermute(term, 'sec', [(0, 1), (1, 0)])  2.63 us
    ppermute x1, starting transfers between devices, shards(): other = lax.ppermute(term, 'sec', [(0, 1), (1, 0)])  1.91 us
    pallas_call x1, Pallas kernels, shards(): pl.pallas_call(sum_kernel, out_shape=pltpu.HBM((boxes, cols, width), jnp....  1.4 us
  transfers between devices with their start and end apart: 1, of which 1 were waited for; matrix products, arithmetic and copies ran while one was open for 0% of the time, Pallas kernels for 0%

profile of v11, /device:TPU:451, one launch (start us, length us, event | category | flops | bytes accessed | tf_op | source)
XLA Modules:
  0.0 66.9 jit_solution(4004633530984002647)
XLA Ops:
  0.0 61.0 %conditional.1 = (bf16[16,128,256]{2,1,0:T(8,128)(2,1)S(1)}) conditional(s32[]{:T(128)} %convert_element_type.3, (bf16[16,128,256]{2,1,0:T(8,128)(2,1)}, bf16[6,32,256]{2,1,0:T(8,128)(2,1)}, s32[16,6]{0,1:T(8,128)}, s32[16]{0:T(128)}, f32[16,6,256]{2,0,1:T(8,128)}) %tuple.12, (s32[4,16]{1,0:T(4,128)}, bf16[16,128,256]{2,1,0:T(8,128)(2,1)}, ...), branch_computations={%region_0.0_spmd, %region_1.0_spmd} | conditional | flops 4831838208 | bytes 18516756 | solution.py:212
  0.0 0.0 copy-start.3
  0.0 4.7 %local_levels.1 = bf16[16,128,256]{2,1,0:T(8,128)(2,1)S(1)} custom-call(s32[4,16]{1,0:T(4,128)} %get-tuple-element.48.orders_in, bf16[16,128,256]{2,1,0:T(8,128)(2,1)} %get-tuple-element.32.probes, bf16[9,512,256]{2,1,0:T(8,128)(2,1)} %bitcast.6, f32[4,16,256]{2,1,0:T(8,128)} %get-tuple-element.50.gains_in), custom_call_target="tpu_custom_call" | custom-call | flops 2147483648 | bytes 2097152 | tf_op jit(solution)/shard_map/cond/branch_1_fun/local_levels/pallas_call | solution.py:148
  4.7 27.5 %all_to_all.12.rows = bf16[32,64,256]{2,1,0:T(8,128)(2,1)S(1)} all-to-all(bf16[32,64,256]{2,1,0:T(8,128)(2,1)S(1)} %bitcast.4), channel_id=1, replica_groups=mesh['bfly'=32,'sec'=2,'probe'=8] {'bfly'}, dimensions={0} | all-to-all | bytes 2097152 | tf_op jit(solution)/shard_map/cond/branch_1_fun/all_to_all | solution.py:167
  32.2 0.0 copy-done.3
  32.2 2.9 %cross_levels.1 = bf16[32,64,256]{2,1,0:T(8,128)(2,1)S(1)} custom-call(bf16[32,64,256]{2,1,0:T(8,128)(2,1)S(1)} %all_to_all.12.rows, bf16[9,512,256]{2,1,0:T(8,128)(2,1)S(1)} %bitcast.7), custom_call_target="tpu_custom_call" | custom-call | flops 2684354560 | bytes 2097152 | tf_op jit(solution)/shard_map/cond/branch_1_fun/cross_levels/pallas_call | solution.py:168
  35.1 25.8 %all_to_all.13 = bf16[32,64,256]{2,1,0:T(8,128)(2,1)S(1)} all-to-all(bf16[32,64,256]{2,1,0:T(8,128)(2,1)S(1)} %cross_levels.1), channel_id=1, replica_groups=mesh['bfly'=32,'sec'=2,'probe'=8] {'bfly'}, dimensions={0} | all-to-all | bytes 2097152 | tf_op jit(solution)/shard_map/cond/branch_1_fun/all_to_all | solution.py:178
  61.0 1.9 %collective-permute-start.2 = (bf16[16,128,256]{2,1,0:T(8,128)(2,1)S(1)}, bf16[16,128,256]{2,1,0:T(8,128)(2,1)S(1)}, u32[]{:S(2)}, u32[]{:S(2)}) collective-permute-start(bf16[16,128,256]{2,1,0:T(8,128)(2,1)S(1)} %get-tuple-element.59.mine), channel_id=1, source_target_pairs={{0,8},{8,0},{1,9},{9,1},{2,10},{10,2},{3,11},{11,3},{4,12},{12,4},... | collective-permute-start | bytes 3145736 | tf_op jit(solution)/shard_map/ppermute | solution.py:213
  62.9 2.6 %collective-permute-done.2.other = bf16[16,128,256]{2,1,0:T(8,128)(2,1)S(1)} collective-permute-done((bf16[16,128,256]{2,1,0:T(8,128)(2,1)S(1)}, bf16[16,128,256]{2,1,0:T(8,128)(2,1)S(1)}, u32[]{:S(2)}, u32[]{:S(2)}) %collective-permute-start.2) | collective-permute-done | bytes 1048608 | tf_op jit(solution)/shard_map/ppermute | solution.py:213
  65.5 1.4 %response_sum.1 = f32[16,128,256]{2,1,0:T(8,128)} custom-call(bf16[16,128,256]{2,1,0:T(8,128)(2,1)S(1)} %get-tuple-element.59.mine, bf16[16,128,256]{2,1,0:T(8,128)(2,1)S(1)} %collective-permute-done.2.other), custom_call_target="tpu_custom_call" | custom-call | flops 1048576 | bytes 4194304 | tf_op jit(solution)/shard_map/response_sum/pallas_call | solution.py:215
Async XLA Ops:
  0.0 32.2 %copy-start.3 = (bf16[9,2,256,256]{3,2,1,0:T(8,128)(2,1)S(1)}, bf16[9,2,256,256]{3,2,1,0:T(8,128)(2,1)}, u32[]{:S(2)}) copy-start(bf16[9,2,256,256]{3,2,1,0:T(8,128)(2,1)} %get-tuple-element.51) | copy-start | bytes 7077892 | tf_op jit(solution)/shard_map/cond
  61.0 4.5 %collective-permute-start.2 = (bf16[16,128,256]{2,1,0:T(8,128)(2,1)S(1)}, bf16[16,128,256]{2,1,0:T(8,128)(2,1)S(1)}, u32[]{:S(2)}, u32[]{:S(2)}) collective-permute-start(bf16[16,128,256]{2,1,0:T(8,128)(2,1)S(1)} %get-tuple-element.59.mine), channel_id=1, source_target_pairs={{0,8},{8,0},{1,9},{9,1},{2,10},{10,2},{3,11},{11,3},{4,12},{12,4},... | collective-permute-start | bytes 3145736 | tf_op jit(solution)/shard_map/ppermute | solution.py:213
